TPU v7x, 128 devices: a whole 4x4x4 slice. The times are simulated.
128 devices in a mesh: frames: 16 (over y, z_hi, core), mp: 8 (over z_lo, x).
Axes of the slice: x: 4, y: 4, z: 4 (z_hi: 2, z_lo: 2; z = z_hi * 2 + z_lo), core: 2. Of those that a mesh axis runs over, the one named last changes fastest.
Arguments:
- teacher_states: bfloat16 [65536, 1024], P('frames', 'mp'), may hold values from -6 to 6
- teacher_pred: bfloat16 [16384, 1024], P(('frames', 'mp')), may hold values from -6 to 6
- teacher_out: bfloat16 [1024, 1024], replicated, may hold values from -0.9 to 0.9
- student_states: bfloat16 [65536, 512], P(('frames', 'mp')), may hold values from -6 to 6
- embed_last: bfloat16 [1024, 512], replicated, may hold values from -4.1875 to 4.1875
- embed_second: bfloat16 [1024, 512], replicated, may hold values from -4.1875 to 4.1875
- student_out: bfloat16 [512, 1024], replicated, may hold values from -1.26 to 1.26
- labels: int32 [16384], P(('frames', 'mp')), may hold values from 1 to 1023
- label_utt: int32 [16384], P(('frames', 'mp')), may hold values from 0 to 340, never falling along the last dimension, each value on 1 to 96 neighbouring positions
- band_start: int32 [2048], P(('frames', 'mp')), may hold values from 0 to 124, as said below
- block_list: int32 [128, 16], P(('frames', 'mp')), may hold values from 0 to 2047, as said below
Outputs:
- divergence: float32 [2048, 4, 32], P(('frames', 'mp'))
Inputs may be any that keep to these rules, and one draw needn't show every extreme that they name: `band_start`: within a device the starts do not fall from block to block. `block_list`: every block is listed exactly once; an owner lists only blocks of devices with its own mp index; at most 2 blocks of one device are listed by one owner, and some owner lists 2 from one device.
All inputs are finite; a program needn't handle non-finite values.
Results may differ from a plain program's by a relative error of at most 0.0045.
Values may be sent and summed in bfloat16 or wider, within the bound.
No kernel may reach another device: no remote copies, remote signals or barrier semaphores. Data moves between devices by JAX's collectives and lax.ppermute only.
A program may use at most 128 MiB of HBM per device.

v0:
```python
import jax
import jax.numpy as jnp
from jax import lax
from jax.experimental import pallas as pl
from jax.experimental.pallas import tpu as pltpu
from jax.sharding import PartitionSpec as P

S = 4
CAP = 2
LANES = 128
TAG_ROWS = 16
GROUP = 4
BF16 = jnp.bfloat16
F32 = jnp.float32


def shifted_2(block, axis, distance):
    devices = range(lax.axis_size(axis))
    route = [(i - distance, i) for i in devices if i - distance in devices]
    return lax.ppermute(block, axis, route)


def by_lanes(pred):
    return pred.astype(F32).reshape(pred.shape[0], -1, LANES)


def vmem():
    return pl.BlockSpec(memory_space=pltpu.VMEM)


def smem():
    return pl.BlockSpec(memory_space=pltpu.SMEM)


def pack(block_list, student_states, frame_peers, blocks_per_peer):
    count = block_list.shape[1]
    rows, width = student_states.shape
    block_rows = rows // count
    pieces = width // LANES
    slot_rows = block_rows * pieces
    message = CAP * slot_rows + TAG_ROWS

    def body(list_ref, states_ref, out_ref, used):
        lane = lax.broadcasted_iota(jnp.int32, (TAG_ROWS, LANES), 1)
        for peer in range(frame_peers):
            used[peer] = 0
            out_ref[peer, CAP * slot_rows :, :] = jnp.full((TAG_ROWS, LANES), -1.0, BF16)
        for j in range(count):
            block = list_ref[0, j]
            peer = block // blocks_per_peer
            slot = used[peer]
            used[peer] = slot + 1
            local = block % count
            for piece in range(pieces):
                at = pl.multiple_of(slot * slot_rows + piece * block_rows, TAG_ROWS)
                out_ref[peer, pl.ds(at, block_rows), :] = states_ref[
                    j * block_rows : (j + 1) * block_rows, piece * LANES : (piece + 1) * LANES
                ]
            tags = out_ref[peer, CAP * slot_rows :, :].astype(F32)
            tags = jnp.where(lane == slot, local.astype(F32), tags)
            out_ref[peer, CAP * slot_rows :, :] = tags.astype(BF16)

    return pl.pallas_call(
        body,
        out_shape=jax.ShapeDtypeStruct((frame_peers, message, LANES), BF16),
        in_specs=[smem(), vmem()],
        out_specs=vmem(),
        scratch_shapes=[pltpu.SMEM((frame_peers,), jnp.int32)],
        compiler_params=pltpu.CompilerParams(vmem_limit_bytes=60 << 20),
        cost_estimate=pl.CostEstimate(flops=0, bytes_accessed=3 << 20, transcendentals=0),
        name="pack",
    )(block_list, student_states)


def teacher(relaid, teacher_pred, teacher_out, band_start):
    pieces, rows, _ = relaid.shape
    count = band_start.shape[0]
    width, vocab = teacher_out.shape
    block_rows = rows // count
    out_block = S * block_rows
    step_rows = GROUP * out_block

    def body(start_ref, states_ref, pred_ref, weight_ref, e_ref, stat_ref, act):
        step = pl.program_id(0)
        for local in range(GROUP):
            first = start_ref[step * GROUP + local]
            for piece in range(pieces):
                cols = slice(piece * LANES, (piece + 1) * LANES)
                states = states_ref[piece, local * block_rows : (local + 1) * block_rows, :].astype(F32)
                for k in range(S):
                    at = local * out_block + k * block_rows
                    band = pred_ref[first + k, piece : piece + 1, :]
                    act[at : at + block_rows, cols] = jnp.tanh(states + band).astype(BF16)
        logits = jnp.dot(act[...], weight_ref[...], preferred_element_type=F32)
        shifted = logits - jnp.max(logits, axis=-1, keepdims=True)
        e = jnp.exp(shifted)
        e_ref[...] = e
        total = jnp.sum(e, axis=-1, keepdims=True)
        weighted = jnp.sum(e * shifted, axis=-1, keepdims=True)
        lane = lax.broadcasted_iota(jnp.int32, (step_rows, LANES), 1)
        inverse = 1.0 / total
        stat_ref[...] = jnp.where(lane == 0, inverse, weighted * inverse - jnp.log(total))

    return pl.pallas_call(
        body,
        grid=(count // GROUP,),
        out_shape=(
            jax.ShapeDtypeStruct((count * out_block, vocab), F32),
            jax.ShapeDtypeStruct((count * out_block, LANES), F32),
        ),
        in_specs=[
            smem(),
            pl.BlockSpec((pieces, GROUP * block_rows, LANES), lambda i: (0, i, 0)),
            pl.BlockSpec(teacher_pred.shape, lambda i: (0, 0, 0)),
            pl.BlockSpec((width, vocab), lambda i: (0, 0)),
        ],
        out_specs=(
            pl.BlockSpec((step_rows, vocab), lambda i: (i, 0)),
            pl.BlockSpec((step_rows, LANES), lambda i: (i, 0)),
        ),
        scratch_shapes=[pltpu.VMEM((step_rows, width), BF16)],
        compiler_params=pltpu.CompilerParams(vmem_limit_bytes=60 << 20),
        cost_estimate=pl.CostEstimate(
            flops=2 * count * out_block * width * vocab,
            bytes_accessed=14 << 20,
            transcendentals=count * out_block * (width + vocab),
        ),
        name="teacher",
    )(band_start, relaid, teacher_pred, teacher_out)


def student(arrived, student_pred, student_out, band_start, e, stats):
    peers, message, _ = arrived.shape
    count = band_start.shape[0]
    width, vocab = student_out.shape
    pieces = width // LANES
    slot_rows = (message - TAG_ROWS) // CAP
    block_rows = slot_rows // pieces
    out_block = S * block_rows
    step_rows = GROUP * out_block
    assert out_block == LANES

    def body(
        start_ref, arrived_ref, pred_ref, weight_ref, e_ref, stat_ref, out_ref,
        act, tags, tag_smem, where, answers, sem,
    ):
        step = pl.program_id(0)

        @pl.when(step == 0)
        def _():
            for peer in range(peers):
                tile = arrived_ref[peer, CAP * slot_rows :, :].astype(F32)
                tags[peer : peer + 1, :] = tile[:1, :].astype(jnp.int32)
            copy = pltpu.make_async_copy(tags, tag_smem, sem)
            copy.start()
            copy.wait()
            for peer in range(peers):
                for slot in range(CAP):
                    block = tag_smem[peer, slot]
                    where[jnp.where(block < 0, count, block)] = peer * CAP + slot

        for local in range(GROUP):
            block = step * GROUP + local
            first = start_ref[block]
            place = where[block]
            peer = place // CAP
            slot = place % CAP
            for piece in range(pieces):
                cols = slice(piece * LANES, (piece + 1) * LANES)
                at = pl.multiple_of(slot * slot_rows + piece * block_rows, TAG_ROWS)
                states = arrived_ref[peer, pl.ds(at, block_rows), :].astype(F32)
                for k in range(S):
                    at = local * out_block + k * block_rows
                    band = pred_ref[first + k, piece : piece + 1, :]
                    act[at : at + block_rows, cols] = jnp.tanh(states + band).astype(BF16)
        logits = jnp.dot(act[...], weight_ref[...], preferred_element_type=F32)
        shifted = logits - jnp.max(logits, axis=-1, keepdims=True)
        total = jnp.sum(jnp.exp(shifted), axis=-1, keepdims=True)
        cross = jnp.sum(e_ref[...] * shifted, axis=-1, keepdims=True)
        answer = stat_ref[:, 1:2] - cross * stat_ref[:, 0:1] + jnp.log(total)
        lane = lax.broadcasted_iota(jnp.int32, (LANES, LANES), 1)
        for local in range(GROUP):
            column = answer[local * out_block : (local + 1) * out_block, :]
            answers[...] = jnp.where(lane == step * GROUP + local, column, answers[...])

        @pl.when(step == count // GROUP - 1)
        def _():
            answers[...] = answers[...].T
            for block in range(count):
                place = where[block]
                out_ref[place // CAP, place % CAP] = jnp.broadcast_to(answers[block : block + 1, :], (8, LANES))

    return pl.pallas_call(
        body,
        grid=(count // GROUP,),
        out_shape=jax.ShapeDtypeStruct((peers, CAP, 8, LANES), F32),
        in_specs=[
            smem(),
            pl.BlockSpec((peers, message, LANES), lambda i: (0, 0, 0)),
            pl.BlockSpec(student_pred.shape, lambda i: (0, 0, 0)),
            pl.BlockSpec((width, vocab), lambda i: (0, 0)),
            pl.BlockSpec((step_rows, vocab), lambda i: (i, 0)),
            pl.BlockSpec((step_rows, LANES), lambda i: (i, 0)),
        ],
        out_specs=pl.BlockSpec((peers, CAP, 8, LANES), lambda i: (0, 0, 0, 0)),
        scratch_shapes=[
            pltpu.VMEM((step_rows, width), BF16),
            pltpu.VMEM((peers, LANES), jnp.int32),
            pltpu.SMEM((peers, LANES), jnp.int32),
            pltpu.SMEM((count + 1,), jnp.int32),
            pltpu.VMEM((LANES, LANES), F32),
            pltpu.SemaphoreType.DMA,
        ],
        compiler_params=pltpu.CompilerParams(vmem_limit_bytes=60 << 20),
        cost_estimate=pl.CostEstimate(
            flops=2 * count * out_block * width * vocab,
            bytes_accessed=12 << 20,
            transcendentals=count * out_block * (width + vocab),
        ),
        name="student",
    )(band_start, arrived, student_pred, student_out, e, stats)


def pick(block_list, answers, blocks_per_peer, block_rows):
    count = block_list.shape[1]
    peers = answers.shape[0]

    def body(list_ref, answers_ref, out_ref, used, rows):
        for peer in range(peers):
            used[peer] = 0
        for j in range(count):
            peer = list_ref[0, j] // blocks_per_peer
            slot = used[peer]
            used[peer] = slot + 1
            rows[j : j + 1, :] = answers_ref[peer, slot, :1, :]
        for k in range(S):
            out_ref[:, k, :] = rows[:, k * block_rows : (k + 1) * block_rows]

    return pl.pallas_call(
        body,
        out_shape=jax.ShapeDtypeStruct((count, S, block_rows), F32),
        in_specs=[smem(), vmem()],
        out_specs=vmem(),
        scratch_shapes=[pltpu.SMEM((peers,), jnp.int32), pltpu.VMEM((count, LANES), F32)],
        compiler_params=pltpu.CompilerParams(vmem_limit_bytes=60 << 20),
        name="pick",
    )(block_list, answers)


def shards(
    teacher_states,
    teacher_pred,
    teacher_out,
    student_states,
    embed_last,
    embed_second,
    student_out,
    labels,
    label_utt,
    band_start,
    block_list,
):
    block_count = band_start.shape[0]
    block_rows = student_states.shape[0] // block_count
    frame_peers = lax.axis_size("frames")
    mp_peers = lax.axis_size("mp")
    blocks_per_peer = block_count * mp_peers

    relaid = lax.all_to_all(
        teacher_states.reshape(mp_peers, -1, teacher_states.shape[1]), "mp", split_axis=0, concat_axis=0
    )
    outgoing = pack(block_list, student_states, frame_peers, blocks_per_peer)
    arrived = lax.all_to_all(outgoing, "frames", split_axis=0, concat_axis=0)

    neighbour = shifted_2(jnp.stack([labels[-2:], label_utt[-2:]]), ("frames", "mp"), 1)
    padded_labels = jnp.concatenate([neighbour[0], labels])
    padded_utts = jnp.concatenate([neighbour[1], label_utt])
    label_count = labels.shape[0]
    last_ctx = jnp.where(
        padded_utts[1 : label_count + 1] == label_utt, padded_labels[1 : label_count + 1], 0
    )
    second_ctx = jnp.where(padded_utts[:label_count] == label_utt, padded_labels[:label_count], 0)
    vocab_ids = jnp.arange(embed_last.shape[0], dtype=jnp.int32)
    last_hot = (last_ctx[:, None] == vocab_ids[None, :]).astype(BF16)
    second_hot = (second_ctx[:, None] == vocab_ids[None, :]).astype(BF16)
    student_pred = (
        jnp.dot(last_hot, embed_last, preferred_element_type=F32)
        + jnp.dot(second_hot, embed_second, preferred_element_type=F32)
    ).astype(BF16)

    e, stats = teacher(relaid, by_lanes(teacher_pred), teacher_out, band_start)
    answers = student(arrived, by_lanes(student_pred), student_out, band_start, e, stats)
    returned = lax.all_to_all(answers, "frames", split_axis=0, concat_axis=0)
    return pick(block_list, returned, blocks_per_peer, block_rows)


def solution(mesh):
    placed = (
        P("frames", "mp"),
        P(("frames", "mp"), None),
        P(),
        P(("frames", "mp"), None),
        P(),
        P(),
        P(),
        P(("frames", "mp")),
        P(("frames", "mp")),
        P(("frames", "mp")),
        P(("frames", "mp"), None),
    )
    return jax.shard_map(
        shards,
        mesh=mesh,
        in_specs=placed,
        out_specs=P(("frames", "mp"), None, None),
        check_vma=False,
    )
```

profile of v0, /device:TPU:1, one launch (start us, length us, event | category | flops | bytes accessed | tf_op | source)
XLA Modules:
  0.0 75.3 jit_solution(13016932183839415700)
XLA Ops:
  0.0 0.0 copy-start
  0.0 0.0 copy-start.6
  0.0 0.0 copy-start.5
  0.0 0.0 copy-start.4
  0.0 6.3 %all-to-all-start.1 = ((bf16[8,512,128]{2,1,0:T(8,128)(2,1)}), bf16[8,512,128]{2,1,0:T(8,128)(2,1)S(1)}, u32[]{:S(2)}, u32[]{:S(2)}) async-start(bf16[8,512,128]{2,1,0:T(8,128)(2,1)} %bitcast.14), calls=%async_computation.1 | async-start | bytes 2097152 | tf_op jit(solution)/shard_map/all_to_all | solution.py:269
  6.4 0.0 copy-done.6
  6.4 0.0 copy-done.5
  6.4 0.1 slice_bitcast_fusion.2
  6.5 3.4 %collective-permute-start = (s32[2,2]{1,0:T(2,128)S(1)}, s32[2,2]{1,0:T(2,128)S(1)}, u32[]{:S(2)}, u32[]{:S(2)}) collective-permute-start(s32[2,2]{1,0:T(2,128)S(1)} %pad_add_fusion), channel_id=1, source_target_pairs={{0,1},{1,2},{2,3},{3,4},{4,5},{5,6},{6,7},{7,8},{8,9},{9,10},{10,1... | collective-permute-start | bytes 56 | tf_op jit(solution)/shard_map/ppermute | solution.py:20
  9.8 0.0 copy-done.4
  9.9 0.9 %copy.12 = f32[16,8,8,128]{3,2,1,0:T(8,128)} copy(f32[16,8,8,128]{3,1,2,0:T(8,128)S(1)} %convert_bitcast_fusion) | data formatting | bytes 1048576
  10.8 2.4 %pack.1 = bf16[16,272,128]{2,1,0:T(8,128)(2,1)} custom-call(s32[1,16]{1,0:T(1,128)} %list_ref.3, bf16[512,512]{1,0:T(8,128)(2,1)} %states_ref.1), custom_call_target="tpu_custom_call" | custom-call | bytes 3145728 | tf_op jit(solution)/shard_map/pack/pallas_call | solution.py:63
  13.1 0.0 copy-start.2
  13.1 9.5 %collective-permute-done = s32[2,2]{1,0:T(2,128)S(1)} collective-permute-done((s32[2,2]{1,0:T(2,128)S(1)}, s32[2,2]{1,0:T(2,128)S(1)}, u32[]{:S(2)}, u32[]{:S(2)}) %collective-permute-start) | collective-permute-done | bytes 48 | tf_op jit(solution)/shard_map/ppermute | solution.py:20
  22.6 0.1 pad_add_fusion.1
  22.7 0.1 pad_add_fusion.2
  22.8 0.0 all-to-all-done.1.states_ref
  22.8 0.0 copy-start.3
  22.8 1.0 %copy-done.3 = bf16[8,512,128]{2,1,0:T(8,128)(2,1)} copy-done((bf16[8,512,128]{2,1,0:T(8,128)(2,1)}, bf16[8,512,128]{2,1,0:T(8,128)(2,1)S(1)}, u32[]{:S(2)}) %copy-start.3) | copy-done | bytes 1048600
  23.8 7.7 %all-to-all-start = ((bf16[16,272,128]{2,1,0:T(8,128)(2,1)}), bf16[16,272,128]{2,1,0:T(8,128)(2,1)S(1)}, u32[]{:S(2)}, u32[]{:S(2)}) async-start(bf16[16,272,128]{2,1,0:T(8,128)(2,1)} %pack.1), calls=%async_computation | async-start | bytes 2228224 | tf_op jit(solution)/shard_map/all_to_all | solution.py:273
  31.5 0.1 compare_select_fusion
  31.6 0.0 copy-done
  31.6 0.3 fusion.2
  31.9 0.0 copy-done.2
  31.9 0.4 fusion.1
  32.3 0.8 %reshape.21.pred_ref = f32[128,4,128]{2,1,0:T(4,128)} reshape(f32[128,512]{1,0:T(8,128)S(1)} %fusion.1) | data formatting | bytes 524288 | tf_op jit(solution)/shard_map/reshape | solution.py:24
  33.1 10.5 %teacher.1 = (f32[2048,1024]{1,0:T(8,128)}, f32[2048,128]{1,0:T(8,128)}) custom-call(s32[16]{0:T(128)} %start_ref.3, bf16[8,512,128]{2,1,0:T(8,128)(2,1)} %copy-done.3, f32[128,8,128]{2,1,0:T(8,128)} %bitcast.15, bf16[1024,1024]{1,0:T(8,128)(2,1)} %weight_ref.2), custom_call_target="tpu_custom_call" | custom-call | flops 4294967296 | bytes 14680064 | tf_op jit(solution)/shard_map/teacher/pallas_call | solution.py:104
  43.6 5.9 %all-to-all-done.arrived_ref = bf16[16,272,128]{2,1,0:T(8,128)(2,1)S(1)} async-done(((bf16[16,272,128]{2,1,0:T(8,128)(2,1)}), bf16[16,272,128]{2,1,0:T(8,128)(2,1)S(1)}, u32[]{:S(2)}, u32[]{:S(2)}) %all-to-all-start) | async-done | bytes 1114144 | tf_op jit(solution)/shard_map/all_to_all | solution.py:273
  49.4 0.0 copy-start.1
  49.4 1.1 %copy-done.1 = bf16[16,272,128]{2,1,0:T(8,128)(2,1)} copy-done((bf16[16,272,128]{2,1,0:T(8,128)(2,1)}, bf16[16,272,128]{2,1,0:T(8,128)(2,1)S(1)}, u32[]{:S(2)}) %copy-start.1) | copy-done | bytes 1114136
  50.5 10.5 %student.1 = f32[16,2,8,128]{3,2,1,0:T(8,128)} custom-call(s32[16]{0:T(128)} %start_ref.3, bf16[16,272,128]{2,1,0:T(8,128)(2,1)} %copy-done.1, f32[128,4,128]{2,1,0:T(4,128)} %reshape.21.pred_ref, bf16[512,1024]{1,0:T(8,128)(2,1)} %weight_ref.3, f32[2048,1024]{1,0:T(8,128)} %get-tuple-element.7.e_ref, f32[2048,128]{1,0:T(8,128)} %get-tuple-element.8.stat_ref), custom_call_target="tpu_custom_call" | custom-call | flops 2147483648 | bytes 12582912 | tf_op jit(solution)/shard_map/student/pallas_call | solution.py:193
  61.0 12.6 %all_to_all.15.answers_ref = f32[16,2,8,128]{3,2,1,0:T(8,128)} all-to-all(f32[16,2,8,128]{3,2,1,0:T(8,128)} %student.1), channel_id=1, replica_groups=mesh['frames'=16,'mp'=8] {'frames'}, dimensions={0} | all-to-all | bytes 262144 | tf_op jit(solution)/shard_map/all_to_all | solution.py:293
  73.6 1.7 %pick.1 = f32[16,4,32]{2,1,0:T(4,128)} custom-call(s32[1,16]{1,0:T(1,128)} %list_ref.3, f32[16,2,8,128]{3,2,1,0:T(8,128)} %all_to_all.15.answers_ref), custom_call_target="tpu_custom_call" | custom-call | tf_op jit(solution)/shard_map/pick/pallas_call | solution.py:239
  (3 shorter events, 0.1 us)
Async XLA Ops:
  0.0 31.6 %copy-start = (bf16[1024,512]{1,0:T(8,128)(2,1)S(1)}, bf16[1024,512]{1,0:T(8,128)(2,1)}, u32[]{:S(2)}) copy-start(bf16[1024,512]{1,0:T(8,128)(2,1)} %param.15) | copy-start | bytes 3145732
  0.0 6.4 %copy-start.6 = (s32[128]{0:T(128)S(1)}, s32[128]{0:T(128)}, u32[]{:S(2)}) copy-start(s32[128]{0:T(128)} %param.18) | copy-start | bytes 1540
  0.0 6.4 %copy-start.5 = (s32[128]{0:T(128)S(1)}, s32[128]{0:T(128)}, u32[]{:S(2)}) copy-start(s32[128]{0:T(128)} %param.19) | copy-start | bytes 1540
  0.0 9.8 %copy-start.4 = (bf16[128,1024]{1,0:T(8,128)(2,1)S(1)}, bf16[128,1024]{1,0:T(8,128)(2,1)}, u32[]{:S(2)}) copy-start(bf16[128,1024]{1,0:T(8,128)(2,1)} %param.12) | copy-start | bytes 786436
  0.0 22.8 %all-to-all-start.1 = ((bf16[8,512,128]{2,1,0:T(8,128)(2,1)}), bf16[8,512,128]{2,1,0:T(8,128)(2,1)S(1)}, u32[]{:S(2)}, u32[]{:S(2)}) async-start(bf16[8,512,128]{2,1,0:T(8,128)(2,1)} %bitcast.14), calls=%async_computation.1 | async-start | bytes 2097152 | tf_op jit(solution)/shard_map/all_to_all | solution.py:269
  6.5 16.2 %collective-permute-start = (s32[2,2]{1,0:T(2,128)S(1)}, s32[2,2]{1,0:T(2,128)S(1)}, u32[]{:S(2)}, u32[]{:S(2)}) collective-permute-start(s32[2,2]{1,0:T(2,128)S(1)} %pad_add_fusion), channel_id=1, source_target_pairs={{0,1},{1,2},{2,3},{3,4},{4,5},{5,6},{6,7},{7,8},{8,9},{9,10},{10,1... | collective-permute-start | bytes 56 | tf_op jit(solution)/shard_map/ppermute | solution.py:20
  13.1 18.8 %copy-start.2 = (bf16[1024,512]{1,0:T(8,128)(2,1)S(1)}, bf16[1024,512]{1,0:T(8,128)(2,1)}, u32[]{:S(2)}) copy-start(bf16[1024,512]{1,0:T(8,128)(2,1)} %param.16) | copy-start | bytes 3145732
  22.8 1.0 %copy-start.3 = (bf16[8,512,128]{2,1,0:T(8,128)(2,1)}, bf16[8,512,128]{2,1,0:T(8,128)(2,1)S(1)}, u32[]{:S(2)}) copy-start(bf16[8,512,128]{2,1,0:T(8,128)(2,1)S(1)} %all-to-all-done.1.states_ref) | copy-start | bytes 3145732
  23.8 25.6 %all-to-all-start = ((bf16[16,272,128]{2,1,0:T(8,128)(2,1)}), bf16[16,272,128]{2,1,0:T(8,128)(2,1)S(1)}, u32[]{:S(2)}, u32[]{:S(2)}) async-start(bf16[16,272,128]{2,1,0:T(8,128)(2,1)} %pack.1), calls=%async_computation | async-start | bytes 2228224 | tf_op jit(solution)/shard_map/all_to_all | solution.py:273
  49.4 1.1 %copy-start.1 = (bf16[16,272,128]{2,1,0:T(8,128)(2,1)}, bf16[16,272,128]{2,1,0:T(8,128)(2,1)S(1)}, u32[]{:S(2)}) copy-start(bf16[16,272,128]{2,1,0:T(8,128)(2,1)S(1)} %all-to-all-done.arrived_ref) | copy-start | bytes 3342340
where the time goes:
time: 75.7 us; the launch traced here: 75.3 us
  Pallas kernels  25 us (33%)
  starting transfers between devices  17.4 us (23%)
  waiting for transfers between devices  15.4 us (20%)
  blocking collectives  12.6 us (17%)
  local copies, waits for them, and re-layouts  3.81 us (5%)
    all_to_all x1, blocking collectives, shards(): returned = lax.all_to_all(answers, 'frames', split_axis=0, concat_axis=0)  12.6 us
    pallas_call x1, Pallas kernels, teacher(): pl.pallas_call(body, grid=(count // GROUP,), out_shape=(jax.ShapeDtypeStr...  10.5 us
    pallas_call x1, Pallas kernels, student(): pl.pallas_call(body, grid=(count // GROUP,), out_shape=jax.ShapeDtypeStru...  10.5 us
    ppermute x1, waiting for transfers between devices, shifted_2(): return lax.ppermute(block, axis, route)  9.5 us
    all_to_all x1, starting transfers between devices, shards(): arrived = lax.all_to_all(outgoing, 'frames', split_axis=0, concat_axis=0)  7.73 us
    all_to_all x1, starting transfers between devices, shards(): lax.all_to_all(teacher_states.reshape(mp_peers, -1, teacher_states.shape[...  6.35 us
    all_to_all x1, waiting for transfers between devices, shards(): arrived = lax.all_to_all(outgoing, 'frames', split_axis=0, concat_axis=0)  5.86 us
    ppermute x1, starting transfers between devices, shifted_2(): return lax.ppermute(block, axis, route)  3.35 us
  transfers between devices with their start and end apart: 3, of which 2 were waited for; matrix products, arithmetic and copies ran while one was open for 4% of the time, Pallas kernels for 17%

commit v1 on v0

v1 whole, which is shorter than its diff:
```python
import jax
import jax.numpy as jnp
from jax import lax
from jax.experimental import pallas as pl
from jax.experimental.pallas import tpu as pltpu
from jax.sharding import PartitionSpec as P

S = 4
CAP = 2
LANES = 128
TAG_ROWS = 16
GROUP = 2
BF16 = jnp.bfloat16
F32 = jnp.float32


def shifted_2(block, axis, distance):
    devices = range(lax.axis_size(axis))
    route = [(i - distance, i) for i in devices if i - distance in devices]
    return lax.ppermute(block, axis, route)


def by_lanes(pred):
    return pred.astype(F32).reshape(pred.shape[0], -1, LANES)


def vmem():
    return pl.BlockSpec(memory_space=pltpu.VMEM)


def hbm():
    return pl.BlockSpec(memory_space=pltpu.HBM)


def anywhere():
    return pl.BlockSpec(memory_space=pl.ANY)


def smem():
    return pl.BlockSpec(memory_space=pltpu.SMEM)


def pack(block_list, student_states, frame_peers, blocks_per_peer):
    count = block_list.shape[1]
    rows, width = student_states.shape
    block_rows = rows // count
    pieces = width // LANES
    slot_rows = block_rows * pieces
    message = CAP * slot_rows + TAG_ROWS

    def body(list_ref, states_ref, out_ref, used):
        lane = lax.broadcasted_iota(jnp.int32, (TAG_ROWS, LANES), 1)
        for peer in range(frame_peers):
            used[peer] = 0
            out_ref[peer, CAP * slot_rows :, :] = jnp.full((TAG_ROWS, LANES), -1.0, BF16)
        for j in range(count):
            block = list_ref[0, j]
            peer = block // blocks_per_peer
            slot = used[peer]
            used[peer] = slot + 1
            local = block % count
            for piece in range(pieces):
                at = pl.multiple_of(slot * slot_rows + piece * block_rows, TAG_ROWS)
                out_ref[peer, pl.ds(at, block_rows), :] = states_ref[
                    j * block_rows : (j + 1) * block_rows, piece * LANES : (piece + 1) * LANES
                ]
            tags = out_ref[peer, CAP * slot_rows :, :].astype(F32)
            tags = jnp.where(lane == slot, local.astype(F32), tags)
            out_ref[peer, CAP * slot_rows :, :] = tags.astype(BF16)

    return pl.pallas_call(
        body,
        out_shape=jax.ShapeDtypeStruct((frame_peers, message, LANES), BF16),
        in_specs=[smem(), vmem()],
        out_specs=vmem(),
        scratch_shapes=[pltpu.SMEM((frame_peers,), jnp.int32)],
        compiler_params=pltpu.CompilerParams(vmem_limit_bytes=4 << 20),
        cost_estimate=pl.CostEstimate(flops=0, bytes_accessed=3 << 20, transcendentals=0),
        name="pack",
    )(block_list, student_states)


def teacher(relaid, teacher_pred, teacher_out, student_out_t, band_start):
    pieces, rows, _ = relaid.shape
    count = band_start.shape[0]
    width, vocab = teacher_out.shape
    student_width = student_out_t.shape[1]
    block_rows = rows // count
    out_block = S * block_rows
    step_rows = GROUP * out_block
    steps = count // GROUP
    total_rows = count * out_block

    def body(start_ref, states_ref, pred_ref, weight_ref, student_ref, q_ref, stat_ref, act, logits, e, inverse, sums, cross):
        lane = lax.broadcasted_iota(jnp.int32, (out_block, LANES), 1)

        def activate(step):
            for block in range(step * GROUP, (step + 1) * GROUP):
                first = start_ref[block]
                for piece in range(pieces):
                    cols = slice(piece * LANES, (piece + 1) * LANES)
                    states = states_ref[piece, block * block_rows : (block + 1) * block_rows, :].astype(F32)
                    for k in range(S):
                        at = block * out_block + k * block_rows
                        band = pred_ref[first + k, piece : piece + 1, :]
                        act[at : at + block_rows, cols] = jnp.tanh(states + band).astype(BF16)

        def multiply(step):
            at = slice(step * step_rows, (step + 1) * step_rows)
            logits[at, :] = jnp.dot(act[at, :], weight_ref[...], preferred_element_type=F32)

        def normalise(step):
            for block in range(step * GROUP, (step + 1) * GROUP):
                at = slice(block * out_block, (block + 1) * out_block)
                values = logits[at, :]
                shifted = values - jnp.max(values, axis=-1, keepdims=True)
                exps = jnp.exp(shifted)
                e[at, :] = exps.astype(BF16)
                total = jnp.sum(exps, axis=-1, keepdims=True)
                weighted = jnp.sum(exps * shifted, axis=-1, keepdims=True)
                inverse[at, :] = jnp.broadcast_to(1.0 / total, (out_block, LANES))
                sums[...] = jnp.where(lane == block, total, sums[...])
                cross[...] = jnp.where(lane == block, weighted, cross[...])

        def project(step):
            at = slice(step * step_rows, (step + 1) * step_rows)
            product = jnp.dot(e[at, :], student_ref[...], preferred_element_type=F32)
            scale = inverse[at, :]
            for piece in range(student_width // LANES):
                cols = slice(piece * LANES, (piece + 1) * LANES)
                q_ref[at, cols] = (product[:, cols] * scale).astype(BF16)

        for step in range(steps + 3):
            for delay, part in enumerate((activate, multiply, normalise, project)):
                if 0 <= step - delay < steps:
                    part(step - delay)
        total = sums[...].T[:count]
        stat_ref[...] = cross[...].T[:count] / total - jnp.log(total)

    return pl.pallas_call(
        body,
        out_shape=(
            jax.ShapeDtypeStruct((total_rows, student_width), BF16),
            jax.ShapeDtypeStruct((count, out_block), F32),
        ),
        in_specs=[smem(), vmem(), vmem(), vmem(), vmem()],
        out_specs=(vmem(), vmem()),
        scratch_shapes=[
            pltpu.VMEM((total_rows, width), BF16),
            pltpu.VMEM((total_rows, vocab), F32),
            pltpu.VMEM((total_rows, vocab), BF16),
            pltpu.VMEM((total_rows, LANES), F32),
            pltpu.VMEM((out_block, LANES), F32),
            pltpu.VMEM((out_block, LANES), F32),
        ],
        compiler_params=pltpu.CompilerParams(vmem_limit_bytes=56 << 20),
        cost_estimate=pl.CostEstimate(
            flops=2 * total_rows * (width + student_width) * vocab,
            bytes_accessed=8 << 20,
            transcendentals=total_rows * (width + vocab),
        ),
        name="teacher",
    )(band_start, relaid, teacher_pred, teacher_out, student_out_t)


def student(arrived, student_pred, student_out, band_start, q, stats):
    peers, message, _ = arrived.shape
    count = band_start.shape[0]
    width, vocab = student_out.shape
    pieces = width // LANES
    slot_rows = (message - TAG_ROWS) // CAP
    block_rows = slot_rows // pieces
    out_block = S * block_rows
    step_rows = GROUP * out_block
    steps = count // GROUP
    total_rows = count * out_block
    assert out_block == LANES

    def body(
        start_ref, arrived_ref, pred_hbm, weight_hbm, q_hbm, stat_ref, out_ref,
        act, logits, products, pred_ref, weight_ref, q_ref, tags, tag_smem, where, sums, cross, sems,
    ):
        lane = lax.broadcasted_iota(jnp.int32, (out_block, LANES), 1)
        copies = [
            pltpu.make_async_copy(pred_hbm, pred_ref, sems.at[1]),
            pltpu.make_async_copy(weight_hbm, weight_ref, sems.at[2]),
            pltpu.make_async_copy(q_hbm, q_ref, sems.at[3]),
        ]
        for each in copies:
            each.start()
        for peer in range(peers):
            tile = arrived_ref[peer, CAP * slot_rows :, :].astype(F32)
            tags[peer : peer + 1, :] = tile[:1, :].astype(jnp.int32)
        copy = pltpu.make_async_copy(tags, tag_smem, sems.at[0])
        copy.start()
        copy.wait()
        for peer in range(peers):
            for slot in range(CAP):
                block = tag_smem[peer, slot]
                where[jnp.where(block < 0, count, block)] = peer * CAP + slot

        for each in copies:
            each.wait()

        def activate(step):
            for block in range(step * GROUP, (step + 1) * GROUP):
                first = start_ref[block]
                place = where[block]
                peer = place // CAP
                slot = place % CAP
                terms = [None] * S
                for piece in range(pieces):
                    cols = slice(piece * LANES, (piece + 1) * LANES)
                    at = pl.multiple_of(slot * slot_rows + piece * block_rows, TAG_ROWS)
                    states = arrived_ref[peer, pl.ds(at, block_rows), :].astype(F32)
                    for k in range(S):
                        at = block * out_block + k * block_rows
                        band = pred_ref[first + k, piece : piece + 1, :]
                        values = jnp.tanh(states + band).astype(BF16)
                        act[at : at + block_rows, cols] = values
                        term = values.astype(F32) * q_ref[at : at + block_rows, cols].astype(F32)
                        terms[k] = term if terms[k] is None else terms[k] + term
                for k in range(S):
                    at = block * out_block + k * block_rows
                    products[at : at + block_rows, :] = terms[k]

        def multiply(step):
            at = slice(step * step_rows, (step + 1) * step_rows)
            logits[at, :] = jnp.dot(act[at, :], weight_ref[...], preferred_element_type=F32)

        def normalise(step):
            for block in range(step * GROUP, (step + 1) * GROUP):
                at = slice(block * out_block, (block + 1) * out_block)
                values = logits[at, :]
                largest = jnp.max(values, axis=-1, keepdims=True)
                total = jnp.sum(jnp.exp(values - largest), axis=-1, keepdims=True)
                mixed = jnp.sum(products[at, :], axis=-1, keepdims=True)
                sums[...] = jnp.where(lane == block, total, sums[...])
                cross[...] = jnp.where(lane == block, largest - mixed, cross[...])

        for step in range(steps + 2):
            for delay, part in enumerate((activate, multiply, normalise)):
                if 0 <= step - delay < steps:
                    part(step - delay)
        answers = stat_ref[...] + cross[...].T[:count] + jnp.log(sums[...].T[:count])
        for block in range(count):
            place = where[block]
            out_ref[place // CAP, place % CAP] = jnp.broadcast_to(answers[block : block + 1, :], (8, LANES))

    return pl.pallas_call(
        body,
        out_shape=jax.ShapeDtypeStruct((peers, CAP, 8, LANES), F32),
        in_specs=[smem(), vmem(), anywhere(), anywhere(), anywhere(), vmem()],
        out_specs=vmem(),
        scratch_shapes=[
            pltpu.VMEM((total_rows, width), BF16),
            pltpu.VMEM((total_rows, vocab), F32),
            pltpu.VMEM((total_rows, LANES), F32),
            pltpu.VMEM(student_pred.shape, F32),
            pltpu.VMEM((width, vocab), BF16),
            pltpu.VMEM((total_rows, width), BF16),
            pltpu.VMEM((peers, LANES), jnp.int32),
            pltpu.SMEM((peers, LANES), jnp.int32),
            pltpu.SMEM((count + 1,), jnp.int32),
            pltpu.VMEM((out_block, LANES), F32),
            pltpu.VMEM((out_block, LANES), F32),
            pltpu.SemaphoreType.DMA((4,)),
        ],
        compiler_params=pltpu.CompilerParams(vmem_limit_bytes=50 << 20),
        cost_estimate=pl.CostEstimate(
            flops=2 * total_rows * width * vocab,
            bytes_accessed=6 << 20,
            transcendentals=total_rows * (width + vocab),
        ),
        name="student",
    )(band_start, arrived, student_pred, student_out, q, stats)


def pick(block_list, answers, blocks_per_peer, block_rows):
    count = block_list.shape[1]
    peers = answers.shape[0]

    def body(list_ref, answers_ref, out_ref, used, rows):
        for peer in range(peers):
            used[peer] = 0
        for j in range(count):
            peer = list_ref[0, j] // blocks_per_peer
            slot = used[peer]
            used[peer] = slot + 1
            rows[j : j + 1, :] = answers_ref[peer, slot, :1, :]
        for k in range(S):
            out_ref[:, k, :] = rows[:, k * block_rows : (k + 1) * block_rows]

    return pl.pallas_call(
        body,
        out_shape=jax.ShapeDtypeStruct((count, S, block_rows), F32),
        in_specs=[smem(), vmem()],
        out_specs=vmem(),
        scratch_shapes=[pltpu.SMEM((peers,), jnp.int32), pltpu.VMEM((count, LANES), F32)],
        compiler_params=pltpu.CompilerParams(vmem_limit_bytes=4 << 20),
        name="pick",
    )(block_list, answers)


def shards(
    teacher_states,
    teacher_pred,
    teacher_out,
    student_states,
    embed_last,
    embed_second,
    student_out,
    labels,
    label_utt,
    band_start,
    block_list,
):
    block_count = band_start.shape[0]
    block_rows = student_states.shape[0] // block_count
    frame_peers = lax.axis_size("frames")
    mp_peers = lax.axis_size("mp")
    blocks_per_peer = block_count * mp_peers

    relaid = lax.all_to_all(
        teacher_states.reshape(mp_peers, -1, teacher_states.shape[1]), "mp", split_axis=0, concat_axis=0
    )
    outgoing = pack(block_list, student_states, frame_peers, blocks_per_peer)
    arrived = lax.all_to_all(outgoing, "frames", split_axis=0, concat_axis=0)

    neighbour = shifted_2(jnp.stack([labels[-2:], label_utt[-2:]]), ("frames", "mp"), 1)
    padded_labels = jnp.concatenate([neighbour[0], labels])
    padded_utts = jnp.concatenate([neighbour[1], label_utt])
    label_count = labels.shape[0]
    last_ctx = jnp.where(
        padded_utts[1 : label_count + 1] == label_utt, padded_labels[1 : label_count + 1], 0
    )
    second_ctx = jnp.where(padded_utts[:label_count] == label_utt, padded_labels[:label_count], 0)
    vocab_ids = jnp.arange(embed_last.shape[0], dtype=jnp.int32)
    last_hot = (last_ctx[:, None] == vocab_ids[None, :]).astype(BF16)
    second_hot = (second_ctx[:, None] == vocab_ids[None, :]).astype(BF16)
    student_pred = (
        jnp.dot(last_hot, embed_last, preferred_element_type=F32)
        + jnp.dot(second_hot, embed_second, preferred_element_type=F32)
    ).astype(BF16)

    q, stats = teacher(relaid, by_lanes(teacher_pred), teacher_out, student_out.T, band_start)
    answers = student(arrived, by_lanes(student_pred), student_out, band_start, q, stats)
    returned = lax.all_to_all(answers, "frames", split_axis=0, concat_axis=0)
    return pick(block_list, returned, blocks_per_peer, block_rows)


def solution(mesh):
    placed = (
        P("frames", "mp"),
        P(("frames", "mp"), None),
        P(),
        P(("frames", "mp"), None),
        P(),
        P(),
        P(),
        P(("frames", "mp")),
        P(("frames", "mp")),
        P(("frames", "mp")),
        P(("frames", "mp"), None),
    )
    return jax.shard_map(
        shards,
        mesh=mesh,
        in_specs=placed,
        out_specs=P(("frames", "mp"), None, None),
        check_vma=False,
    )
```

time: 75.7 us -> 69.6 us (0.919)
  waiting for transfers between devices: 15.4 us -> 11.2 us
  Pallas kernels: 25 us -> 21.2 us
  matrix products: 0.7 us -> 2.62 us
    all_to_all x1, waiting for transfers between devices: 5.86 us -> 2.49 us  [shards(): arrived = lax.all_to_all(outgoing, 'frames', split_axis=0, concat_axis=0)]
    pallas_call x2, Pallas kernels: 20.9 us -> 18 us  [the longest x1 11.7 us: teacher(): pl.pallas_call(body, out_shape=(jax.ShapeDtypeStruct((total_rows, student...]
    dot_general x1, matrix products: 0.35 us -> 2.27 us  [shards(): jnp.dot(second_hot, embed_second, preferred_element_type=F32)]
    ppermute x1, waiting for transfers between devices: 9.5 us -> 8.71 us  [shifted_2(): return lax.ppermute(block, axis, route)]
    unnamed x15 -> x20, local copies, waits for them, and re-layouts: 2.96 us -> 2.95 us
  transfers between devices with their start and end apart: 3 -> 3, of which waited for: 2 -> 2; matrix products, arithmetic and copies ran while one was open for 4% -> 9% of each run, Pallas kernels for 17% -> 20%
where the time goes in v1:
time: 69.6 us; the launch traced here: 69.2 us
  Pallas kernels  21.2 us (30%)
  starting transfers between devices  17.5 us (25%)
  blocking collectives  12.2 us (18%)
  waiting for transfers between devices  11.2 us (16%)
  local copies, waits for them, and re-layouts  4.06 us (6%)
  matrix products  2.62 us (4%)
    all_to_all x1, blocking collectives, shards(): returned = lax.all_to_all(answers, 'frames', split_axis=0, concat_axis=0)  12.2 us
    pallas_call x1, Pallas kernels, teacher(): pl.pallas_call(body, out_shape=(jax.ShapeDtypeStruct((total_rows, student...  11.7 us
    ppermute x1, waiting for transfers between devices, shifted_2(): return lax.ppermute(block, axis, route)  8.71 us
    all_to_all x1, starting transfers between devices, shards(): arrived = lax.all_to_all(outgoing, 'frames', split_axis=0, concat_axis=0)  7.66 us
    all_to_all x1, starting transfers between devices, shards(): lax.all_to_all(teacher_states.reshape(mp_peers, -1, teacher_states.shape[...  6.35 us
    pallas_call x1, Pallas kernels, student(): pl.pallas_call(body, out_shape=jax.ShapeDtypeStruct((peers, CAP, 8, LANES...  6.3 us
    ppermute x1, starting transfers between devices, shifted_2(): return lax.ppermute(block, axis, route)  3.49 us
    unnamed x20, local copies, waits for them, and re-layouts  2.95 us
  transfers between devices with their start and end apart: 3, of which 2 were waited for; matrix products, arithmetic and copies ran while one was open for 9% of the time, Pallas kernels for 20%

profile of v1, /device:TPU:1, one launch (start us, length us, event | category | flops | bytes accessed | tf_op | source)
XLA Modules:
  0.0 69.2 jit_solution(5015024731026122931)
XLA Ops:
  0.0 0.0 copy-start
  0.0 0.0 copy-start.7
  0.0 0.0 copy-start.8
  0.0 0.0 copy-start.6
  0.0 0.0 copy-start.1
  0.0 6.3 %all-to-all-start.1 = ((bf16[8,512,128]{2,1,0:T(8,128)(2,1)}), bf16[8,512,128]{2,1,0:T(8,128)(2,1)}, u32[]{:S(2)}, u32[]{:S(2)}) async-start(bf16[8,512,128]{2,1,0:T(8,128)(2,1)} %bitcast.15), calls=%async_computation.1 | async-start | bytes 2097152 | tf_op jit(solution)/shard_map/all_to_all | solution.py:324
  6.4 0.0 copy-done.7
  6.4 0.0 copy-done.8
  6.4 0.0 copy-start.2
  6.4 0.0 copy-start.3
  6.4 0.1 slice_bitcast_fusion.2
  6.5 3.5 %collective-permute-start = (s32[2,2]{1,0:T(2,128)S(1)}, s32[2,2]{1,0:T(2,128)S(1)}, u32[]{:S(2)}, u32[]{:S(2)}) collective-permute-start(s32[2,2]{1,0:T(2,128)S(1)} %pad_add_fusion), channel_id=1, source_target_pairs={{0,1},{1,2},{2,3},{3,4},{4,5},{5,6},{6,7},{7,8},{8,9},{9,10},{10,1... | collective-permute-start | bytes 56 | tf_op jit(solution)/shard_map/ppermute | solution.py:20
  10.0 0.0 copy-done.6
  10.1 0.9 %copy.13 = f32[16,8,8,128]{3,2,1,0:T(8,128)} copy(f32[16,8,8,128]{3,1,2,0:T(8,128)S(1)} %convert_bitcast_fusion) | data formatting | bytes 1048576
  11.0 0.0 copy-done.1
  11.0 1.3 %copy.12 = bf16[512,1024]{0,1:T(8,128)(2,1)} copy(bf16[512,1024]{1,0:T(8,128)(2,1)S(1)} %copy-done.1) | data formatting | bytes 2097152 | tf_op args[6]
  12.3 0.0 copy-done.2
  12.3 0.0 copy-done.3
  12.3 1.8 %pack.1 = bf16[16,272,128]{2,1,0:T(8,128)(2,1)} custom-call(s32[1,16]{1,0:T(1,128)S(1)} %copy-done.3, bf16[512,512]{1,0:T(8,128)(2,1)S(1)} %copy-done.2), custom_call_target="tpu_custom_call" | custom-call | bytes 3145728 | tf_op jit(solution)/shard_map/pack/pallas_call | solution.py:71
  14.0 8.7 %collective-permute-done = s32[2,2]{1,0:T(2,128)S(1)} collective-permute-done((s32[2,2]{1,0:T(2,128)S(1)}, s32[2,2]{1,0:T(2,128)S(1)}, u32[]{:S(2)}, u32[]{:S(2)}) %collective-permute-start) | collective-permute-done | bytes 48 | tf_op jit(solution)/shard_map/ppermute | solution.py:20
  22.8 0.1 pad_add_fusion.1
  22.8 0.1 pad_add_fusion.2
  22.9 0.1 compare_select_fusion
  23.0 0.0 all-to-all-done.1.states_ref
  23.0 7.7 %all-to-all-start = ((bf16[16,272,128]{2,1,0:T(8,128)(2,1)}), bf16[16,272,128]{2,1,0:T(8,128)(2,1)S(1)}, u32[]{:S(2)}, u32[]{:S(2)}) async-start(bf16[16,272,128]{2,1,0:T(8,128)(2,1)} %pack.1), calls=%async_computation | async-start | bytes 2228224 | tf_op jit(solution)/shard_map/all_to_all | solution.py:328
  30.7 0.0 copy-done
  30.7 0.3 fusion.2
  31.0 2.3 %fusion.1 = f32[128,512]{1,0:T(8,128)} fusion(f32[128,512]{1,0:T(8,128)S(1)} %fusion.2, bf16[1024,512]{1,0:T(8,128)(2,1)} %param.16, s32[128]{0:T(128)S(1)} %get-tuple-element.9), kind=kOutput, calls=%fused_computation.2 | convolution fusion | flops 134545408 | bytes 1573376 | tf_op jit(solution)/shard_map/dot_general | solution.py:343
  33.3 1.0 %reshape.21.pred_hbm = f32[128,4,128]{2,1,0:T(4,128)S(1)} reshape(f32[128,512]{1,0:T(8,128)} %fusion.1) | data formatting | bytes 524288 | tf_op jit(solution)/shard_map/reshape | solution.py:24
  34.3 0.0 copy-start.4
  34.3 11.7 %teacher.1 = (bf16[2048,512]{1,0:T(8,128)(2,1)}, f32[16,128]{1,0:T(8,128)}) custom-call(s32[16]{0:T(128)} %start_ref.3, bf16[8,512,128]{2,1,0:T(8,128)(2,1)} %all-to-all-done.1.states_ref, f32[128,8,128]{2,1,0:T(8,128)} %bitcast.17, bf16[1024,1024]{1,0:T(8,128)(2,1)} %weight_ref.1, bf16[1024,512]{1,0:T(8,128)(2,1)} %bitcast.16), custom_call_target="tpu_custom_call" | custom-call | flops 6442450944 | bytes 8388608 | tf_op jit(solution)/shard_map/teacher/pallas_call | solution.py:140
  46.1 2.5 %all-to-all-done.arrived_ref = bf16[16,272,128]{2,1,0:T(8,128)(2,1)S(1)} async-done(((bf16[16,272,128]{2,1,0:T(8,128)(2,1)}), bf16[16,272,128]{2,1,0:T(8,128)(2,1)S(1)}, u32[]{:S(2)}, u32[]{:S(2)}) %all-to-all-start) | async-done | bytes 1114144 | tf_op jit(solution)/shard_map/all_to_all | solution.py:328
  48.6 0.0 copy-done.4
  48.6 0.0 copy-start.5
  48.6 0.7 %copy-done.5 = f32[16,128]{1,0:T(8,128)S(1)} copy-done((f32[16,128]{1,0:T(8,128)S(1)}, f32[16,128]{1,0:T(8,128)}, u32[]{:S(2)}) %copy-start.5) | copy-done | bytes 8216
  49.3 6.3 %student.1 = f32[16,2,8,128]{3,2,1,0:T(8,128)S(1)} custom-call(s32[16]{0:T(128)S(1)} %copy-done.4, bf16[16,272,128]{2,1,0:T(8,128)(2,1)S(1)} %all-to-all-done.arrived_ref, f32[128,4,128]{2,1,0:T(4,128)S(1)} %reshape.21.pred_hbm, bf16[512,1024]{1,0:T(8,128)(2,1)S(1)} %copy-done.1, bf16[2048,512]{1,0:T(8,128)(2,1)} %get-tuple-element.7.q_hbm, ...), custom_call_target="tpu_custom_call" | custom-call | flops 2147483648 | bytes 6291456 | tf_op jit(solution)/shard_map/student/pallas_call | solution.py:250
  55.6 12.2 %all_to_all.15.answers_ref = f32[16,2,8,128]{3,2,1,0:T(8,128)S(1)} all-to-all(f32[16,2,8,128]{3,2,1,0:T(8,128)S(1)} %student.1), channel_id=1, replica_groups=mesh['frames'=16,'mp'=8] {'frames'}, dimensions={0} | all-to-all | bytes 262144 | tf_op jit(solution)/shard_map/all_to_all | solution.py:348
  67.8 1.4 %pick.1 = f32[16,4,32]{2,1,0:T(4,128)} custom-call(s32[1,16]{1,0:T(1,128)S(1)} %copy-done.3, f32[16,2,8,128]{3,2,1,0:T(8,128)S(1)} %all_to_all.15.answers_ref), custom_call_target="tpu_custom_call" | custom-call | tf_op jit(solution)/shard_map/pick/pallas_call | solution.py:294
  (3 shorter events, 0.1 us)
Async XLA Ops:
  0.0 30.7 %copy-start = (bf16[1024,512]{1,0:T(8,128)(2,1)S(1)}, bf16[1024,512]{1,0:T(8,128)(2,1)}, u32[]{:S(2)}) copy-start(bf16[1024,512]{1,0:T(8,128)(2,1)} %param.15) | copy-start | bytes 3145732
  0.0 6.4 %copy-start.7 = (s32[128]{0:T(128)S(1)}, s32[128]{0:T(128)}, u32[]{:S(2)}) copy-start(s32[128]{0:T(128)} %param.19) | copy-start | bytes 1540
  0.0 6.4 %copy-start.8 = (s32[128]{0:T(128)S(1)}, s32[128]{0:T(128)}, u32[]{:S(2)}) copy-start(s32[128]{0:T(128)} %param.18) | copy-start | bytes 1540
  0.0 10.0 %copy-start.6 = (bf16[128,1024]{1,0:T(8,128)(2,1)S(1)}, bf16[128,1024]{1,0:T(8,128)(2,1)}, u32[]{:S(2)}) copy-start(bf16[128,1024]{1,0:T(8,128)(2,1)} %param.12) | copy-start | bytes 786436
  0.0 10.9 %copy-start.1 = (bf16[512,1024]{1,0:T(8,128)(2,1)S(1)}, bf16[512,1024]{1,0:T(8,128)(2,1)}, u32[]{:S(2)}) copy-start(bf16[512,1024]{1,0:T(8,128)(2,1)} %weight_hbm.1) | copy-start | bytes 3145732
  0.0 23.0 %all-to-all-start.1 = ((bf16[8,512,128]{2,1,0:T(8,128)(2,1)}), bf16[8,512,128]{2,1,0:T(8,128)(2,1)}, u32[]{:S(2)}, u32[]{:S(2)}) async-start(bf16[8,512,128]{2,1,0:T(8,128)(2,1)} %bitcast.15), calls=%async_computation.1 | async-start | bytes 2097152 | tf_op jit(solution)/shard_map/all_to_all | solution.py:324
  6.4 5.9 %copy-start.2 = (bf16[512,512]{1,0:T(8,128)(2,1)S(1)}, bf16[512,512]{1,0:T(8,128)(2,1)}, u32[]{:S(2)}) copy-start(bf16[512,512]{1,0:T(8,128)(2,1)} %states_ref.1) | copy-start | bytes 1572868
  6.4 5.9 %copy-start.3 = (s32[1,16]{1,0:T(1,128)S(1)}, s32[1,16]{1,0:T(1,128)}, u32[]{:S(2)}) copy-start(s32[1,16]{1,0:T(1,128)} %list_ref.3) | copy-start | bytes 196
  6.5 16.3 %collective-permute-start = (s32[2,2]{1,0:T(2,128)S(1)}, s32[2,2]{1,0:T(2,128)S(1)}, u32[]{:S(2)}, u32[]{:S(2)}) collective-permute-start(s32[2,2]{1,0:T(2,128)S(1)} %pad_add_fusion), channel_id=1, source_target_pairs={{0,1},{1,2},{2,3},{3,4},{4,5},{5,6},{6,7},{7,8},{8,9},{9,10},{10,1... | collective-permute-start | bytes 56 | tf_op jit(solution)/shard_map/ppermute | solution.py:20
  23.0 25.6 %all-to-all-start = ((bf16[16,272,128]{2,1,0:T(8,128)(2,1)}), bf16[16,272,128]{2,1,0:T(8,128)(2,1)S(1)}, u32[]{:S(2)}, u32[]{:S(2)}) async-start(bf16[16,272,128]{2,1,0:T(8,128)(2,1)} %pack.1), calls=%async_computation | async-start | bytes 2228224 | tf_op jit(solution)/shard_map/all_to_all | solution.py:328
  34.3 14.2 %copy-start.4 = (s32[16]{0:T(128)S(1)}, s32[16]{0:T(128)}, u32[]{:S(2)}) copy-start(s32[16]{0:T(128)} %start_ref.3) | copy-start | bytes 196
  48.6 0.7 %copy-start.5 = (f32[16,128]{1,0:T(8,128)S(1)}, f32[16,128]{1,0:T(8,128)}, u32[]{:S(2)}) copy-start(f32[16,128]{1,0:T(8,128)} %get-tuple-element.8.stat_ref) | copy-start | bytes 24580

commit v2 on v1

v2 whole, which is shorter than its diff:
```python
import jax
import jax.numpy as jnp
from jax import lax
from jax.experimental import pallas as pl
from jax.experimental.pallas import tpu as pltpu
from jax.sharding import PartitionSpec as P

S = 4
CAP = 2
LANES = 128
TAG_ROWS = 16
CORES = 2
PARTS = 3
GROUP = 2
BF16 = jnp.bfloat16
F32 = jnp.float32


def shifted_2(block, axis, distance):
    devices = range(lax.axis_size(axis))
    route = [(i - distance, i) for i in devices if i - distance in devices]
    return lax.ppermute(block, axis, route)


def by_tiles(rows, out_ref):
    for piece in range(rows.shape[1] // LANES):
        out_ref[:, piece, :] = rows[:, piece * LANES : (piece + 1) * LANES]


def vmem():
    return pl.BlockSpec(memory_space=pltpu.VMEM)


def hbm():
    return pl.BlockSpec(memory_space=pltpu.HBM)


def anywhere():
    return pl.BlockSpec(memory_space=pl.ANY)


def smem():
    return pl.BlockSpec(memory_space=pltpu.SMEM)


def pack(
    block_list, student_states, core, labels, label_utt, embed_last, embed_second, teacher_pred, student_out,
    frame_peers, blocks_per_peer,
):
    count = block_list.shape[1]
    rows, width = student_states.shape
    block_rows = rows // count
    pieces = width // LANES
    slot_rows = block_rows * pieces
    message = CAP * slot_rows + TAG_ROWS
    chips = frame_peers // CORES
    label_count = labels.shape[1]
    words = embed_last.shape[0]
    assert label_count == LANES

    def body(
        list_ref, core_ref, states_ref, labels_ref, utt_ref, last_ref, second_ref, teacher_pred_ref, student_ref,
        own_ref, other_ref, pred_ref, tiles_ref, turned_ref, used, hot,
    ):
        wide = lax.broadcasted_iota(jnp.int32, (LANES, LANES), 1)

        def embed(distance, ref):
            label = pltpu.roll(jnp.broadcast_to(labels_ref[...], (8, LANES)), distance, 1)
            utt = pltpu.roll(jnp.broadcast_to(utt_ref[...], (8, LANES)), distance, 1)
            label = jnp.where(utt == utt_ref[...], label, 0)
            label = jnp.broadcast_to(label[:1, :].astype(F32), (LANES, LANES)).T.astype(jnp.int32)
            for piece in range(words // LANES):
                cols = slice(piece * LANES, (piece + 1) * LANES)
                hot[:, cols] = (label == wide + piece * LANES).astype(F32).astype(BF16)
            return jnp.dot(hot[...], ref[...], preferred_element_type=F32)

        pred = (embed(1, last_ref) + embed(2, second_ref)).astype(BF16)
        by_tiles(pred.astype(F32), pred_ref)
        by_tiles(teacher_pred_ref[...].astype(F32), tiles_ref)
        turned_ref[...] = student_ref[...].astype(F32).T.astype(BF16)
        lane = lax.broadcasted_iota(jnp.int32, (TAG_ROWS, LANES), 1)
        for peer in range(frame_peers):
            used[peer] = 0
        for chip in range(chips):
            for out_ref in (own_ref, other_ref):
                out_ref[chip, CAP * slot_rows :, :] = jnp.full((TAG_ROWS, LANES), -1.0, BF16)
        for j in range(count):
            block = list_ref[0, j]
            peer = block // blocks_per_peer
            slot = used[peer]
            used[peer] = slot + 1
            local = block % count

            def put(out_ref):
                chip = peer // CORES
                for piece in range(pieces):
                    at = pl.multiple_of(slot * slot_rows + piece * block_rows, TAG_ROWS)
                    out_ref[chip, pl.ds(at, block_rows), :] = states_ref[
                        j * block_rows : (j + 1) * block_rows, piece * LANES : (piece + 1) * LANES
                    ]
                tags = out_ref[chip, CAP * slot_rows :, :].astype(F32)
                tags = jnp.where(lane == slot, local.astype(F32), tags)
                out_ref[chip, CAP * slot_rows :, :] = tags.astype(BF16)

            pl.when(peer % CORES == core_ref[0])(lambda: put(own_ref))
            pl.when(peer % CORES != core_ref[0])(lambda: put(other_ref))

    return pl.pallas_call(
        body,
        out_shape=(jax.ShapeDtypeStruct((chips, message, LANES), BF16),) * 2
        + (
            jax.ShapeDtypeStruct((label_count, pieces, LANES), F32),
            jax.ShapeDtypeStruct((label_count, teacher_pred.shape[1] // LANES, LANES), F32),
            jax.ShapeDtypeStruct(student_out.shape[::-1], BF16),
        ),
        in_specs=[smem(), smem()] + [vmem()] * 7,
        out_specs=(vmem(),) * 5,
        scratch_shapes=[pltpu.SMEM((frame_peers,), jnp.int32), pltpu.VMEM((label_count, words), BF16)],
        compiler_params=pltpu.CompilerParams(vmem_limit_bytes=16 << 20),
        cost_estimate=pl.CostEstimate(flops=0, bytes_accessed=3 << 20, transcendentals=0),
        name="pack",
    )(block_list, core, student_states, labels, label_utt, embed_last, embed_second, teacher_pred, student_out)


def teacher(relaid, teacher_pred, teacher_out, student_out_t, band_start):
    pieces, rows, _ = relaid.shape
    count = band_start.shape[0]
    width, vocab = teacher_out.shape
    student_width = student_out_t.shape[1]
    block_rows = rows // count
    out_block = S * block_rows
    step_rows = GROUP * out_block
    steps = count // GROUP
    total_rows = count * out_block

    def body(start_ref, states_ref, pred_ref, weight_ref, student_ref, q_ref, act, logits, e, inverse, sums, cross):
        lane = lax.broadcasted_iota(jnp.int32, (out_block, LANES), 1)

        def activate(step):
            for block in range(step * GROUP, (step + 1) * GROUP):
                first = start_ref[block]
                for piece in range(pieces):
                    cols = slice(piece * LANES, (piece + 1) * LANES)
                    states = states_ref[piece, block * block_rows : (block + 1) * block_rows, :].astype(F32)
                    for k in range(S):
                        at = block * out_block + k * block_rows
                        band = pred_ref[first + k, piece : piece + 1, :]
                        act[at : at + block_rows, cols] = jnp.tanh(states + band).astype(BF16)

        def multiply(step):
            at = slice(step * step_rows, (step + 1) * step_rows)
            logits[at, :] = jnp.dot(act[at, :], weight_ref[...], preferred_element_type=F32)

        def normalise(step):
            for block in range(step * GROUP, (step + 1) * GROUP):
                at = slice(block * out_block, (block + 1) * out_block)
                values = logits[at, :]
                shifted = values - jnp.max(values, axis=-1, keepdims=True)
                exps = jnp.exp(shifted)
                e[at, :] = exps.astype(BF16)
                total = jnp.sum(exps, axis=-1, keepdims=True)
                weighted = jnp.sum(exps * shifted, axis=-1, keepdims=True)
                inverse[at, :] = jnp.broadcast_to(1.0 / total, (out_block, LANES))
                sums[...] = jnp.where(lane == block, total, sums[...])
                cross[...] = jnp.where(lane == block, weighted, cross[...])

        def project(step):
            at = slice(step * step_rows, (step + 1) * step_rows)
            product = jnp.dot(e[at, :], student_ref[...], preferred_element_type=F32)
            scale = inverse[at, :]
            for piece in range(student_width // LANES):
                cols = slice(piece * LANES, (piece + 1) * LANES)
                q_ref[at, cols] = (product[:, cols] * scale).astype(BF16)

        for step in range(steps + 3):
            for delay, part in enumerate((activate, multiply, normalise, project)):
                if 0 <= step - delay < steps:
                    part(step - delay)
        total = sums[...].T[:count]
        rest = cross[...].T[:count] / total - jnp.log(total)
        for part in range(PARTS):
            rounded = rest.astype(BF16)
            q_ref[total_rows:, part * LANES : (part + 1) * LANES] = rounded
            rest = rest - rounded.astype(F32)

    return pl.pallas_call(
        body,
        out_shape=jax.ShapeDtypeStruct((total_rows + count, student_width), BF16),
        in_specs=[smem(), vmem(), vmem(), vmem(), vmem()],
        out_specs=vmem(),
        scratch_shapes=[
            pltpu.VMEM((total_rows, width), BF16),
            pltpu.VMEM((total_rows, vocab), F32),
            pltpu.VMEM((total_rows, vocab), BF16),
            pltpu.VMEM((total_rows, LANES), F32),
            pltpu.VMEM((out_block, LANES), F32),
            pltpu.VMEM((out_block, LANES), F32),
        ],
        compiler_params=pltpu.CompilerParams(vmem_limit_bytes=56 << 20),
        cost_estimate=pl.CostEstimate(flops=40 << 30, bytes_accessed=8 << 20, transcendentals=0),
        name="teacher",
    )(band_start, relaid, teacher_pred, teacher_out, student_out_t)


def student(
    core, arrived, student_pred, student_out, band_start, q, labels, label_utt, before, embed_last, embed_second
):
    chips, message, _ = arrived.shape
    message //= CORES
    peers = chips * CORES
    count = band_start.shape[0]
    width, vocab = student_out.shape
    pieces = width // LANES
    slot_rows = (message - TAG_ROWS) // CAP
    block_rows = slot_rows // pieces
    out_block = S * block_rows
    step_rows = GROUP * out_block
    steps = count // GROUP
    total_rows = count * out_block
    assert out_block == LANES

    def body(
        start_ref, core_ref, labels_ref, utt_ref, before_ref, arrived_ref, pred_hbm, weight_hbm, q_hbm, last_hbm, second_hbm,
        out_ref, entries,
        act, logits, pred_ref, weight_ref, q_ref, tags, tag_smem, where, sums, cross, sems,
    ):
        lane = lax.broadcasted_iota(jnp.int32, (out_block, LANES), 1)
        copies = [
            pltpu.make_async_copy(pred_hbm, pred_ref, sems.at[1]),
            pltpu.make_async_copy(weight_hbm, weight_ref, sems.at[2]),
            pltpu.make_async_copy(q_hbm, q_ref, sems.at[3]),
        ]
        words = []
        for at in range(2):
            for distance, table in ((1, last_hbm), (2, second_hbm)):
                i = at - distance
                label = labels_ref[i] if i >= 0 else before_ref[0, 2 + i]
                utt = utt_ref[i] if i >= 0 else before_ref[1, 2 + i]
                word = jnp.where(utt == utt_ref[at], label, 0)
                around = pl.multiple_of(word // TAG_ROWS * TAG_ROWS, TAG_ROWS)
                n = len(words)
                words.append(word - around)
                copies.insert(n, pltpu.make_async_copy(table.at[pl.ds(around, TAG_ROWS), :], entries.at[n], sems.at[4 + n]))
        *first_copies, weight_copy, q_copy = copies
        for each in copies:
            each.start()
        for peer in range(peers):
            at = peer % CORES * message + CAP * slot_rows
            tile = arrived_ref[peer // CORES, at : at + TAG_ROWS, :].astype(F32)
            tags[peer : peer + 1, :] = tile[:1, :].astype(jnp.int32)
        copy = pltpu.make_async_copy(tags, tag_smem, sems.at[0])
        copy.start()
        copy.wait()
        for peer in range(peers):
            for slot in range(CAP):
                block = tag_smem[peer, slot]
                where[jnp.where(block < 0, count, block)] = peer * CAP + slot

        for each in first_copies:
            each.wait()
        row = lax.broadcasted_iota(jnp.int32, (TAG_ROWS, width), 0)

        def entry(n):
            return jnp.sum(jnp.where(row == words[n], entries[n].astype(F32), 0.0), axis=0, keepdims=True)

        for at in range(2):
            first_rows = (entry(2 * at) + entry(2 * at + 1)).astype(BF16).astype(F32)
            for piece in range(pieces):
                pred_ref[at, piece : piece + 1, :] = first_rows[:, piece * LANES : (piece + 1) * LANES]

        def activate(step):
            for block in range(step * GROUP, (step + 1) * GROUP):
                first = start_ref[block]
                place = where[block]
                chip = place // (CORES * CAP)
                first_row = place // CAP % CORES * message + place % CAP * slot_rows
                for piece in range(pieces):
                    cols = slice(piece * LANES, (piece + 1) * LANES)
                    at = pl.multiple_of(first_row + piece * block_rows, TAG_ROWS)
                    states = arrived_ref[chip, pl.ds(at, block_rows), :].astype(F32)
                    for k in range(S):
                        at = block * out_block + k * block_rows
                        band = pred_ref[first + k, piece : piece + 1, :]
                        act[at : at + block_rows, cols] = jnp.tanh(states + band).astype(BF16)

        def multiply(step):
            if step == 0:
                weight_copy.wait()
            at = slice(step * step_rows, (step + 1) * step_rows)
            logits[at, :] = jnp.dot(act[at, :], weight_ref[...], preferred_element_type=F32)

        def normalise(step):
            if step == 0:
                q_copy.wait()
            for block in range(step * GROUP, (step + 1) * GROUP):
                at = slice(block * out_block, (block + 1) * out_block)
                values = logits[at, :]
                largest = jnp.max(values, axis=-1, keepdims=True)
                total = jnp.sum(jnp.exp(values - largest), axis=-1, keepdims=True)
                mixed = sum(
                    act[at, piece * LANES : (piece + 1) * LANES].astype(F32)
                    * q_ref[at, piece * LANES : (piece + 1) * LANES].astype(F32)
                    for piece in range(pieces)
                )
                mixed = jnp.sum(mixed, axis=-1, keepdims=True)
                sums[...] = jnp.where(lane == block, total, sums[...])
                cross[...] = jnp.where(lane == block, largest - mixed, cross[...])

        for step in range(steps + 2):
            for delay, part in enumerate((activate, multiply, normalise)):
                if 0 <= step - delay < steps:
                    part(step - delay)
        stats = sum(q_ref[total_rows:, part * LANES : (part + 1) * LANES].astype(F32) for part in range(PARTS))
        answers = stats + cross[...].T[:count] + jnp.log(sums[...].T[:count])
        for block in range(count):
            place = where[block]
            owner = place // (CORES * CAP) * CORES + (place // CAP % CORES + core_ref[0]) % CORES
            out_ref[owner, place % CAP] = jnp.broadcast_to(answers[block : block + 1, :], (8, LANES))

    return pl.pallas_call(
        body,
        out_shape=jax.ShapeDtypeStruct((peers, CAP, 8, LANES), F32),
        in_specs=[smem()] * 5 + [vmem()] + [anywhere()] * 5,
        out_specs=vmem(),
        scratch_shapes=[
            pltpu.VMEM((4, TAG_ROWS, width), BF16),
            pltpu.VMEM((total_rows, width), BF16),
            pltpu.VMEM((total_rows, vocab), F32),
            pltpu.VMEM(student_pred.shape, F32),
            pltpu.VMEM((width, vocab), BF16),
            pltpu.VMEM((total_rows + count, width), BF16),
            pltpu.VMEM((peers, LANES), jnp.int32),
            pltpu.SMEM((peers, LANES), jnp.int32),
            pltpu.SMEM((count + 1,), jnp.int32),
            pltpu.VMEM((out_block, LANES), F32),
            pltpu.VMEM((out_block, LANES), F32),
            pltpu.SemaphoreType.DMA((8,)),
        ],
        compiler_params=pltpu.CompilerParams(vmem_limit_bytes=50 << 20),
        cost_estimate=pl.CostEstimate(
            flops=2 * total_rows * width * vocab,
            bytes_accessed=6 << 20,
            transcendentals=total_rows * (width + vocab),
        ),
        name="student",
    )(
        band_start, core, labels, label_utt, before, arrived, student_pred, student_out, q, embed_last, embed_second
    )


def pick(block_list, answers, blocks_per_peer, block_rows):
    count = block_list.shape[1]
    peers = answers.shape[0]

    def body(list_ref, answers_ref, out_ref, used, rows):
        for peer in range(peers):
            used[peer] = 0
        for j in range(count):
            peer = list_ref[0, j] // blocks_per_peer
            slot = used[peer]
            used[peer] = slot + 1
            rows[j : j + 1, :] = answers_ref[peer, slot, :1, :]
        for k in range(S):
            out_ref[:, k, :] = rows[:, k * block_rows : (k + 1) * block_rows]

    return pl.pallas_call(
        body,
        out_shape=jax.ShapeDtypeStruct((count, S, block_rows), F32),
        in_specs=[smem(), vmem()],
        out_specs=vmem(),
        scratch_shapes=[pltpu.SMEM((peers,), jnp.int32), pltpu.VMEM((count, LANES), F32)],
        compiler_params=pltpu.CompilerParams(vmem_limit_bytes=4 << 20),
        name="pick",
    )(block_list, answers)


def shards(
    teacher_states,
    teacher_pred,
    teacher_out,
    student_states,
    embed_last,
    embed_second,
    student_out,
    labels,
    label_utt,
    band_start,
    block_list,
):
    block_count = band_start.shape[0]
    block_rows = student_states.shape[0] // block_count
    frame_peers = lax.axis_size("frames")
    mp_peers = lax.axis_size("mp")
    blocks_per_peer = block_count * mp_peers

    relaid = lax.all_to_all(
        teacher_states.reshape(mp_peers, -1, teacher_states.shape[1]), "mp", split_axis=0, concat_axis=0
    )
    core = jnp.reshape(lax.axis_index("frames") % CORES, (1,)).astype(jnp.int32)
    own, other, student_pred, teacher_tiles, student_out_t = pack(
        block_list, student_states, core, labels[None], label_utt[None], embed_last, embed_second,
        teacher_pred, student_out, frame_peers, blocks_per_peer,
    )
    other = lax.ppermute(other, "frames", [(i, i ^ 1) for i in range(frame_peers)])
    arrived = lax.all_to_all(
        jnp.concatenate([own, other], axis=1),
        "frames", split_axis=0, concat_axis=0,
        axis_index_groups=[list(range(at, frame_peers, CORES)) for at in range(CORES)],
    )

    before = shifted_2(jnp.stack([labels[-2:], label_utt[-2:]]), ("frames", "mp"), 1)
    q = teacher(relaid, teacher_tiles, teacher_out, student_out_t, band_start)
    answers = student(
        core, arrived, student_pred, student_out, band_start, q, labels, label_utt, before, embed_last, embed_second
    )
    returned = lax.all_to_all(answers, "frames", split_axis=0, concat_axis=0)
    return pick(block_list, returned, blocks_per_peer, block_rows)


def solution(mesh):
    placed = (
        P("frames", "mp"),
        P(("frames", "mp"), None),
        P(),
        P(("frames", "mp"), None),
        P(),
        P(),
        P(),
        P(("frames", "mp")),
        P(("frames", "mp")),
        P(("frames", "mp")),
        P(("frames", "mp"), None),
    )
    return jax.shard_map(
        shards,
        mesh=mesh,
        in_specs=placed,
        out_specs=P(("frames", "mp"), None, None),
        check_vma=False,
    )
```

time: 69.6 us -> 67.4 us (0.968)
  waiting for transfers between devices: 11.2 us -> 8.32 us
  matrix products: 2.62 us -> 0 us
  Pallas kernels: 21.2 us -> 22.3 us
  other arithmetic: 0.28 us -> 1.08 us
  blocking collectives: 12.2 us -> 12.9 us
    ppermute x1, waiting for transfers between devices: 8.71 us -> 0.01 us  [shifted_2(): return lax.ppermute(block, axis, route)]
    all_to_all x1, waiting for transfers between devices: 0.01 us -> 3.78 us  [shards(): lax.all_to_all(teacher_states.reshape(mp_peers, -1, teacher_states.shape[...]
    dot_general x2 -> x0, matrix products: 2.62 us -> none  [the longest x1 2.27 us: shards(): jnp.dot(second_hot, embed_second, preferred_element_type=F32)]
    all_to_all x1, waiting for transfers between devices: 2.49 us -> 4.54 us  [shards(): lax.all_to_all(jnp.concatenate([own, other], axis=1), 'frames', split_axi...]
    unnamed x20 -> x24, local copies, waits for them, and re-layouts: 2.95 us -> 4.05 us
    reshape x1 -> x0, local copies, waits for them, and re-layouts: 1.03 us -> none  [by_lanes(): return pred.astype(F32).reshape(pred.shape[0], -1, LANES)]
    ppermute x0 -> x1, starting transfers between devices: none -> 0.96 us  [shards(): lax.ppermute(other, 'frames', [(i, i ^ 1) for i in range(frame_peers)])]
    concatenate x2 -> x1, other arithmetic: 0.15 us -> 1.06 us  [shards(): jnp.concatenate([own, other], axis=1)]
  transfers between devices with their start and end apart: 3 -> 4, of which waited for: 2 -> 2; matrix products, arithmetic and copies ran while one was open for 9% -> 2% of each run, Pallas kernels for 20% -> 21%
where the time goes in v2:
time: 67.4 us; the launch traced here: 67 us
  Pallas kernels  22.3 us (33%)
  starting transfers between devices  18.1 us (27%)
  blocking collectives  12.9 us (19%)
  waiting for transfers between devices  8.32 us (12%)
  local copies, waits for them, and re-layouts  4.13 us (6%)
  other arithmetic  1.08 us (2%)
    all_to_all x1, blocking collectives, shards(): returned = lax.all_to_all(answers, 'frames', split_axis=0, concat_axis=0)  12.9 us
    pallas_call x1, Pallas kernels, teacher(): pl.pallas_call(body, out_shape=jax.ShapeDtypeStruct((total_rows + count,...  11.8 us
    all_to_all x1, starting transfers between devices, shards(): lax.all_to_all(jnp.concatenate([own, other], axis=1), 'frames', split_axi...  7.21 us
    pallas_call x1, Pallas kernels, student(): pl.pallas_call(body, out_shape=jax.ShapeDtypeStruct((peers, CAP, 8, LANES...  6.85 us
    all_to_all x1, starting transfers between devices, shards(): lax.all_to_all(teacher_states.reshape(mp_peers, -1, teacher_states.shape[...  6.35 us
    all_to_all x1, waiting for transfers between devices, shards(): lax.all_to_all(jnp.concatenate([own, other], axis=1), 'frames', split_axi...  4.54 us
    unnamed x24, local copies, waits for them, and re-layouts  4.05 us
    all_to_all x1, waiting for transfers between devices, shards(): lax.all_to_all(teacher_states.reshape(mp_peers, -1, teacher_states.shape[...  3.78 us
  transfers between devices with their start and end apart: 4, of which 2 were waited for; matrix products, arithmetic and copies ran while one was open for 2% of the time, Pallas kernels for 21%

profile of v2, /device:TPU:1, one launch (start us, length us, event | category | flops | bytes accessed | tf_op | source)
XLA Modules:
  0.0 67.0 jit_solution(7494238525540647576)
XLA Ops:
  0.0 0.0 copy-start.7
  0.0 0.0 copy-start.8
  0.0 0.0 copy-start
  0.0 0.0 copy-start.1
  0.0 0.0 copy-start.6
  0.0 6.3 %all-to-all-start.1 = ((bf16[8,512,128]{2,1,0:T(8,128)(2,1)}), bf16[8,512,128]{2,1,0:T(8,128)(2,1)}, u32[]{:S(2)}, u32[]{:S(2)}) async-start(bf16[8,512,128]{2,1,0:T(8,128)(2,1)} %bitcast.10), calls=%async_computation.1 | async-start | bytes 2097152 | tf_op jit(solution)/shard_map/all_to_all | solution.py:396
  6.4 0.0 copy-done.7
  6.4 0.0 copy-done.8
  6.4 0.0 copy-done
  6.4 0.0 copy-done.1
  6.4 0.0 copy-done.6
  6.4 0.0 copy-start.2
  6.4 1.2 %copy-done.2 = bf16[512,1024]{1,0:T(8,128)(2,1)S(1)} copy-done((bf16[512,1024]{1,0:T(8,128)(2,1)S(1)}, bf16[512,1024]{1,0:T(8,128)(2,1)}, u32[]{:S(2)}) %copy-start.2) | copy-done | bytes 1048600
  7.7 0.0 copy-start.4
  7.7 1.0 %copy-done.4 = bf16[512,512]{1,0:T(8,128)(2,1)S(1)} copy-done((bf16[512,512]{1,0:T(8,128)(2,1)S(1)}, bf16[512,512]{1,0:T(8,128)(2,1)}, u32[]{:S(2)}) %copy-start.4) | copy-done | bytes 524312
  8.7 0.0 copy-start.5
  8.7 0.9 %copy-done.5 = bf16[128,1024]{1,0:T(8,128)(2,1)S(1)} copy-done((bf16[128,1024]{1,0:T(8,128)(2,1)S(1)}, bf16[128,1024]{1,0:T(8,128)(2,1)}, u32[]{:S(2)}) %copy-start.5) | copy-done | bytes 262168
  9.6 2.3 %pack.1 = (bf16[8,272,128]{2,1,0:T(8,128)(2,1)S(1)}, bf16[8,272,128]{2,1,0:T(8,128)(2,1)S(1)}, f32[128,4,128]{2,1,0:T(4,128)S(1)}, f32[128,8,128]{2,1,0:T(8,128)S(1)}, bf16[1024,512]{1,0:T(8,128)(2,1)S(1)}) custom-call(s32[1,16]{1,0:T(1,128)S(1)} %copy-done.6, s32[1]{0:T(128)} %bitcast.core_ref, bf16[512,512]{1,0:T(8,128)(2,1)S(1)} %copy-done.4, ...), custom_call_target="tpu_custom_call" | custom-call | bytes 3145728 | tf_op jit(solution)/shard_map/pack/pallas_call | solution.py:108
  11.9 0.0 copy-start.10
  11.9 0.8 %copy-done.10 = f32[128,8,128]{2,1,0:T(8,128)} copy-done((f32[128,8,128]{2,1,0:T(8,128)}, f32[128,8,128]{2,1,0:T(8,128)S(1)}, u32[]{:S(2)}) %copy-start.10) | copy-done | bytes 524312
  12.8 0.0 copy-start.9
  12.8 1.0 %collective-permute-start.1 = (bf16[8,272,128]{2,1,0:T(8,128)(2,1)S(1)}, bf16[8,272,128]{2,1,0:T(8,128)(2,1)S(1)}, u32[]{:S(2)}, u32[]{:S(2)}) collective-permute-start(bf16[8,272,128]{2,1,0:T(8,128)(2,1)S(1)} %get-tuple-element.11), channel_id=1, source_target_pairs={{0,8},{8,0},{16,24},{24,16},{32,40},{40,32},{48,56},{56,48},{64,72... | collective-permute-start | bytes 1671176 | tf_op jit(solution)/shard_map/ppermute | solution.py:404
  13.7 0.1 slice_bitcast_fusion
  13.8 3.6 %collective-permute-start = (s32[2,2]{1,0:T(2,128)S(1)}, s32[2,2]{1,0:T(2,128)S(1)}, u32[]{:S(2)}, u32[]{:S(2)}) collective-permute-start(s32[2,2]{1,0:T(2,128)S(1)} %pad_add_fusion), channel_id=1, source_target_pairs={{0,1},{1,2},{2,3},{3,4},{4,5},{5,6},{6,7},{7,8},{8,9},{9,10},{10,1... | collective-permute-start | bytes 56 | tf_op jit(solution)/shard_map/ppermute | solution.py:22
  17.4 0.0 collective-permute-done.1
  17.4 1.1 %pad_maximum_fusion = bf16[8,544,128]{2,1,0:T(8,128)(2,1)} fusion(bf16[8,272,128]{2,1,0:T(8,128)(2,1)S(1)} %collective-permute-done.1, bf16[8,272,128]{2,1,0:T(8,128)(2,1)S(1)} %get-tuple-element.10), kind=kLoop, calls=%fused_computation | loop fusion | flops 2228224 | bytes 2228224 | tf_op jit(solution)/shard_map/concatenate | solution.py:406
  18.5 3.8 %all-to-all-done.1.states_ref = bf16[8,512,128]{2,1,0:T(8,128)(2,1)} async-done(((bf16[8,512,128]{2,1,0:T(8,128)(2,1)}), bf16[8,512,128]{2,1,0:T(8,128)(2,1)}, u32[]{:S(2)}, u32[]{:S(2)}) %all-to-all-start.1) | async-done | bytes 1048608 | tf_op jit(solution)/shard_map/all_to_all | solution.py:396
  22.3 0.0 copy-done.9
  22.3 7.2 %all-to-all-start = ((bf16[8,544,128]{2,1,0:T(8,128)(2,1)}), bf16[8,544,128]{2,1,0:T(8,128)(2,1)}, u32[]{:S(2)}, u32[]{:S(2)}) async-start(bf16[8,544,128]{2,1,0:T(8,128)(2,1)} %pad_maximum_fusion), calls=%async_computation | async-start | bytes 2228224 | tf_op jit(solution)/shard_map/all_to_all | solution.py:405
  29.5 0.0 copy-start.3
  29.5 0.0 copy-start.11
  29.5 11.8 %teacher.1.q_hbm = bf16[2064,512]{1,0:T(8,128)(2,1)} custom-call(s32[16]{0:T(128)} %start_ref.3, bf16[8,512,128]{2,1,0:T(8,128)(2,1)} %all-to-all-done.1.states_ref, f32[128,8,128]{2,1,0:T(8,128)} %copy-done.10, bf16[1024,1024]{1,0:T(8,128)(2,1)} %weight_ref.1, bf16[1024,512]{1,0:T(8,128)(2,1)} %copy-done.9), custom_call_target="tpu_custom_call" | custom-call | flops 42949672960 | bytes 8388608 | tf_op jit(solution)/shard_map/teacher/pallas_call | solution.py:186
  41.3 0.0 collective-permute-done.before_ref
  41.3 4.5 %all-to-all-done.arrived_ref = bf16[8,544,128]{2,1,0:T(8,128)(2,1)} async-done(((bf16[8,544,128]{2,1,0:T(8,128)(2,1)}), bf16[8,544,128]{2,1,0:T(8,128)(2,1)}, u32[]{:S(2)}, u32[]{:S(2)}) %all-to-all-start) | async-done | bytes 1114144 | tf_op jit(solution)/shard_map/all_to_all | solution.py:405
  45.8 0.0 copy-done.3
  45.8 0.0 copy-done.11
  45.8 6.8 %student.1 = f32[16,2,8,128]{3,2,1,0:T(8,128)S(1)} custom-call(s32[16]{0:T(128)S(1)} %copy-done.11, s32[1]{0:T(128)} %bitcast.core_ref, s32[128]{0:T(128)S(1)} %copy-done.7, s32[128]{0:T(128)S(1)} %copy-done.8, s32[2,2]{1,0:T(2,128)S(1)} %collective-permute-done.before_ref, bf16[8,544,128]{2,1,0:T(8,128)(2,1)} %all-to-all-done.arrived_ref, ...), custom_call_target="tpu_custom_call" | custom-call | flops 2147483648 | bytes 6291456 | tf_op jit(solution)/shard_map/student/pallas_call | solution.py:320
  52.7 12.9 %all_to_all.15.answers_ref = f32[16,2,8,128]{3,2,1,0:T(8,128)S(1)} all-to-all(f32[16,2,8,128]{3,2,1,0:T(8,128)S(1)} %student.1), channel_id=1, replica_groups=mesh['frames'=16,'mp'=8] {'frames'}, dimensions={0} | all-to-all | bytes 262144 | tf_op jit(solution)/shard_map/all_to_all | solution.py:416
  65.6 1.4 %pick.1 = f32[16,4,32]{2,1,0:T(4,128)} custom-call(s32[1,16]{1,0:T(1,128)S(1)} %copy-done.6, f32[16,2,8,128]{3,2,1,0:T(8,128)S(1)} %all_to_all.15.answers_ref), custom_call_target="tpu_custom_call" | custom-call | tf_op jit(solution)/shard_map/pick/pallas_call | solution.py:366
  (1 shorter events, 0.0 us)
Async XLA Ops:
  0.0 6.4 %copy-start.7 = (s32[128]{0:T(128)S(1)}, s32[128]{0:T(128)}, u32[]{:S(2)}) copy-start(s32[128]{0:T(128)} %labels_ref.1) | copy-start | bytes 1540
  0.0 6.4 %copy-start.8 = (s32[128]{0:T(128)S(1)}, s32[128]{0:T(128)}, u32[]{:S(2)}) copy-start(s32[128]{0:T(128)} %utt_ref.1) | copy-start | bytes 1540
  0.0 6.4 %copy-start = (bf16[1024,512]{1,0:T(8,128)(2,1)S(1)}, bf16[1024,512]{1,0:T(8,128)(2,1)}, u32[]{:S(2)}) copy-start(bf16[1024,512]{1,0:T(8,128)(2,1)} %last_hbm.1) | copy-start | bytes 3145732
  0.0 6.4 %copy-start.1 = (bf16[1024,512]{1,0:T(8,128)(2,1)S(1)}, bf16[1024,512]{1,0:T(8,128)(2,1)}, u32[]{:S(2)}) copy-start(bf16[1024,512]{1,0:T(8,128)(2,1)} %second_hbm.1) | copy-start | bytes 3145732
  0.0 6.4 %copy-start.6 = (s32[1,16]{1,0:T(1,128)S(1)}, s32[1,16]{1,0:T(1,128)}, u32[]{:S(2)}) copy-start(s32[1,16]{1,0:T(1,128)} %list_ref.3) | copy-start | bytes 196
  0.0 22.3 %all-to-all-start.1 = ((bf16[8,512,128]{2,1,0:T(8,128)(2,1)}), bf16[8,512,128]{2,1,0:T(8,128)(2,1)}, u32[]{:S(2)}, u32[]{:S(2)}) async-start(bf16[8,512,128]{2,1,0:T(8,128)(2,1)} %bitcast.10), calls=%async_computation.1 | async-start | bytes 2097152 | tf_op jit(solution)/shard_map/all_to_all | solution.py:396
  6.4 1.2 %copy-start.2 = (bf16[512,1024]{1,0:T(8,128)(2,1)S(1)}, bf16[512,1024]{1,0:T(8,128)(2,1)}, u32[]{:S(2)}) copy-start(bf16[512,1024]{1,0:T(8,128)(2,1)} %weight_hbm.1) | copy-start | bytes 3145732
  7.7 1.0 %copy-start.4 = (bf16[512,512]{1,0:T(8,128)(2,1)S(1)}, bf16[512,512]{1,0:T(8,128)(2,1)}, u32[]{:S(2)}) copy-start(bf16[512,512]{1,0:T(8,128)(2,1)} %states_ref.1) | copy-start | bytes 1572868
  8.7 0.9 %copy-start.5 = (bf16[128,1024]{1,0:T(8,128)(2,1)S(1)}, bf16[128,1024]{1,0:T(8,128)(2,1)}, u32[]{:S(2)}) copy-start(bf16[128,1024]{1,0:T(8,128)(2,1)} %teacher_pred_ref.1) | copy-start | bytes 786436
  11.9 0.8 %copy-start.10 = (f32[128,8,128]{2,1,0:T(8,128)}, f32[128,8,128]{2,1,0:T(8,128)S(1)}, u32[]{:S(2)}) copy-start(f32[128,8,128]{2,1,0:T(8,128)S(1)} %get-tuple-element.13.pred_ref) | copy-start | bytes 1572868
  12.8 9.5 %copy-start.9 = (bf16[1024,512]{1,0:T(8,128)(2,1)}, bf16[1024,512]{1,0:T(8,128)(2,1)S(1)}, u32[]{:S(2)}) copy-start(bf16[1024,512]{1,0:T(8,128)(2,1)S(1)} %get-tuple-element.14.student_ref) | copy-start | bytes 3145732
  12.8 4.7 %collective-permute-start.1 = (bf16[8,272,128]{2,1,0:T(8,128)(2,1)S(1)}, bf16[8,272,128]{2,1,0:T(8,128)(2,1)S(1)}, u32[]{:S(2)}, u32[]{:S(2)}) collective-permute-start(bf16[8,272,128]{2,1,0:T(8,128)(2,1)S(1)} %get-tuple-element.11), channel_id=1, source_target_pairs={{0,8},{8,0},{16,24},{24,16},{32,40},{40,32},{48,56},{56,48},{64,72... | collective-permute-start | bytes 1671176 | tf_op jit(solution)/shard_map/ppermute | solution.py:404
  13.8 27.5 %collective-permute-start = (s32[2,2]{1,0:T(2,128)S(1)}, s32[2,2]{1,0:T(2,128)S(1)}, u32[]{:S(2)}, u32[]{:S(2)}) collective-permute-start(s32[2,2]{1,0:T(2,128)S(1)} %pad_add_fusion), channel_id=1, source_target_pairs={{0,1},{1,2},{2,3},{3,4},{4,5},{5,6},{6,7},{7,8},{8,9},{9,10},{10,1... | collective-permute-start | bytes 56 | tf_op jit(solution)/shard_map/ppermute | solution.py:22
  22.3 23.5 %all-to-all-start = ((bf16[8,544,128]{2,1,0:T(8,128)(2,1)}), bf16[8,544,128]{2,1,0:T(8,128)(2,1)}, u32[]{:S(2)}, u32[]{:S(2)}) async-start(bf16[8,544,128]{2,1,0:T(8,128)(2,1)} %pad_maximum_fusion), calls=%async_computation | async-start | bytes 2228224 | tf_op jit(solution)/shard_map/all_to_all | solution.py:405
  29.5 16.3 %copy-start.3 = (bf16[512,1024]{1,0:T(8,128)(2,1)S(1)}, bf16[512,1024]{1,0:T(8,128)(2,1)}, u32[]{:S(2)}) copy-start(bf16[512,1024]{1,0:T(8,128)(2,1)} %weight_hbm.1) | copy-start | bytes 3145732
  29.5 16.3 %copy-start.11 = (s32[16]{0:T(128)S(1)}, s32[16]{0:T(128)}, u32[]{:S(2)}) copy-start(s32[16]{0:T(128)} %start_ref.3) | copy-start | bytes 196

commit v3 on v2

--- a/solution.py
+++ b/solution.py
@@ -312,14 +312,16 @@
                     part(step - delay)
         stats = sum(q_ref[total_rows:, part * LANES : (part + 1) * LANES].astype(F32) for part in range(PARTS))
         answers = stats + cross[...].T[:count] + jnp.log(sums[...].T[:count])
+        out_ref[...] = jnp.zeros_like(out_ref)
+        slots = lax.broadcasted_iota(jnp.int32, (8, LANES), 0)
         for block in range(count):
             place = where[block]
             owner = place // (CORES * CAP) * CORES + (place // CAP % CORES + core_ref[0]) % CORES
-            out_ref[owner, place % CAP] = jnp.broadcast_to(answers[block : block + 1, :], (8, LANES))
+            out_ref[owner] = jnp.where(slots == place % CAP, answers[block : block + 1, :], out_ref[owner])
 
     return pl.pallas_call(
         body,
-        out_shape=jax.ShapeDtypeStruct((peers, CAP, 8, LANES), F32),
+        out_shape=jax.ShapeDtypeStruct((peers, 8, LANES), F32),
         in_specs=[smem()] * 5 + [vmem()] + [anywhere()] * 5,
         out_specs=vmem(),
         scratch_shapes=[
@@ -353,13 +355,14 @@
     peers = answers.shape[0]
 
     def body(list_ref, answers_ref, out_ref, used, rows):
+        slots = lax.broadcasted_iota(jnp.int32, (8, LANES), 0)
         for peer in range(peers):
             used[peer] = 0
         for j in range(count):
             peer = list_ref[0, j] // blocks_per_peer
             slot = used[peer]
             used[peer] = slot + 1
-            rows[j : j + 1, :] = answers_ref[peer, slot, :1, :]
+            rows[j : j + 1, :] = jnp.sum(jnp.where(slots == slot, answers_ref[peer], 0.0), axis=0, keepdims=True)
         for k in range(S):
             out_ref[:, k, :] = rows[:, k * block_rows : (k + 1) * block_rows]
 

time: 67.4 us -> 67 us (level)
  no operation moved by 1% of the time
where the time goes in v3:
time: 67 us; the launch traced here: 66.6 us
  Pallas kernels  22.2 us (33%)
  starting transfers between devices  18.1 us (27%)
  blocking collectives  12.6 us (19%)
  waiting for transfers between devices  8.31 us (12%)
  local copies, waits for them, and re-layouts  4.13 us (6%)
  other arithmetic  1.08 us (2%)
    all_to_all x1, blocking collectives, shards(): returned = lax.all_to_all(answers, 'frames', split_axis=0, concat_axis=0)  12.6 us
    pallas_call x1, Pallas kernels, teacher(): pl.pallas_call(body, out_shape=jax.ShapeDtypeStruct((total_rows + count,...  11.8 us
    all_to_all x1, starting transfers between devices, shards(): lax.all_to_all(jnp.concatenate([own, other], axis=1), 'frames', split_axi...  7.21 us
    pallas_call x1, Pallas kernels, student(): pl.pallas_call(body, out_shape=jax.ShapeDtypeStruct((peers, 8, LANES), F3...  6.76 us
    all_to_all x1, starting transfers between devices, shards(): lax.all_to_all(teacher_states.reshape(mp_peers, -1, teacher_states.shape[...  6.35 us
    all_to_all x1, waiting for transfers between devices, shards(): lax.all_to_all(jnp.concatenate([own, other], axis=1), 'frames', split_axi...  4.53 us
    unnamed x24, local copies, waits for them, and re-layouts  4.05 us
    all_to_all x1, waiting for transfers between devices, shards(): lax.all_to_all(teacher_states.reshape(mp_peers, -1, teacher_states.shape[...  3.78 us
  transfers between devices with their start and end apart: 4, of which 2 were waited for; matrix products, arithmetic and copies ran while one was open for 2% of the time, Pallas kernels for 21%

profile of v3, /device:TPU:1, one launch (start us, length us, event | category | flops | bytes accessed | tf_op | source)
XLA Modules:
  0.0 66.6 jit_solution(1440258332070764076)
XLA Ops:
  0.0 0.0 copy-start.7
  0.0 0.0 copy-start.8
  0.0 0.0 copy-start
  0.0 0.0 copy-start.1
  0.0 0.0 copy-start.6
  0.0 6.3 %all-to-all-start.1 = ((bf16[8,512,128]{2,1,0:T(8,128)(2,1)}), bf16[8,512,128]{2,1,0:T(8,128)(2,1)}, u32[]{:S(2)}, u32[]{:S(2)}) async-start(bf16[8,512,128]{2,1,0:T(8,128)(2,1)} %bitcast.10), calls=%async_computation.1 | async-start | bytes 2097152 | tf_op jit(solution)/shard_map/all_to_all | solution.py:399
  6.4 0.0 copy-done.7
  6.4 0.0 copy-done.8
  6.4 0.0 copy-done
  6.4 0.0 copy-done.1
  6.4 0.0 copy-done.6
  6.4 0.0 copy-start.2
  6.4 1.2 %copy-done.2 = bf16[512,1024]{1,0:T(8,128)(2,1)S(1)} copy-done((bf16[512,1024]{1,0:T(8,128)(2,1)S(1)}, bf16[512,1024]{1,0:T(8,128)(2,1)}, u32[]{:S(2)}) %copy-start.2) | copy-done | bytes 1048600
  7.7 0.0 copy-start.4
  7.7 1.0 %copy-done.4 = bf16[512,512]{1,0:T(8,128)(2,1)S(1)} copy-done((bf16[512,512]{1,0:T(8,128)(2,1)S(1)}, bf16[512,512]{1,0:T(8,128)(2,1)}, u32[]{:S(2)}) %copy-start.4) | copy-done | bytes 524312
  8.7 0.0 copy-start.5
  8.7 0.9 %copy-done.5 = bf16[128,1024]{1,0:T(8,128)(2,1)S(1)} copy-done((bf16[128,1024]{1,0:T(8,128)(2,1)S(1)}, bf16[128,1024]{1,0:T(8,128)(2,1)}, u32[]{:S(2)}) %copy-start.5) | copy-done | bytes 262168
  9.6 2.3 %pack.1 = (bf16[8,272,128]{2,1,0:T(8,128)(2,1)S(1)}, bf16[8,272,128]{2,1,0:T(8,128)(2,1)S(1)}, f32[128,4,128]{2,1,0:T(4,128)S(1)}, f32[128,8,128]{2,1,0:T(8,128)S(1)}, bf16[1024,512]{1,0:T(8,128)(2,1)S(1)}) custom-call(s32[1,16]{1,0:T(1,128)S(1)} %copy-done.6, s32[1]{0:T(128)} %bitcast.core_ref, bf16[512,512]{1,0:T(8,128)(2,1)S(1)} %copy-done.4, ...), custom_call_target="tpu_custom_call" | custom-call | bytes 3145728 | tf_op jit(solution)/shard_map/pack/pallas_call | solution.py:108
  11.9 0.0 copy-start.10
  11.9 0.8 %copy-done.10 = f32[128,8,128]{2,1,0:T(8,128)} copy-done((f32[128,8,128]{2,1,0:T(8,128)}, f32[128,8,128]{2,1,0:T(8,128)S(1)}, u32[]{:S(2)}) %copy-start.10) | copy-done | bytes 524312
  12.8 0.0 copy-start.9
  12.8 1.0 %collective-permute-start.1 = (bf16[8,272,128]{2,1,0:T(8,128)(2,1)S(1)}, bf16[8,272,128]{2,1,0:T(8,128)(2,1)S(1)}, u32[]{:S(2)}, u32[]{:S(2)}) collective-permute-start(bf16[8,272,128]{2,1,0:T(8,128)(2,1)S(1)} %get-tuple-element.11), channel_id=1, source_target_pairs={{0,8},{8,0},{16,24},{24,16},{32,40},{40,32},{48,56},{56,48},{64,72... | collective-permute-start | bytes 1671176 | tf_op jit(solution)/shard_map/ppermute | solution.py:407
  13.7 0.1 slice_bitcast_fusion
  13.8 3.6 %collective-permute-start = (s32[2,2]{1,0:T(2,128)S(1)}, s32[2,2]{1,0:T(2,128)S(1)}, u32[]{:S(2)}, u32[]{:S(2)}) collective-permute-start(s32[2,2]{1,0:T(2,128)S(1)} %pad_add_fusion), channel_id=1, source_target_pairs={{0,1},{1,2},{2,3},{3,4},{4,5},{5,6},{6,7},{7,8},{8,9},{9,10},{10,1... | collective-permute-start | bytes 56 | tf_op jit(solution)/shard_map/ppermute | solution.py:22
  17.4 0.0 collective-permute-done.1
  17.4 1.1 %pad_maximum_fusion = bf16[8,544,128]{2,1,0:T(8,128)(2,1)} fusion(bf16[8,272,128]{2,1,0:T(8,128)(2,1)S(1)} %collective-permute-done.1, bf16[8,272,128]{2,1,0:T(8,128)(2,1)S(1)} %get-tuple-element.10), kind=kLoop, calls=%fused_computation | loop fusion | flops 2228224 | bytes 2228224 | tf_op jit(solution)/shard_map/concatenate | solution.py:409
  18.5 3.8 %all-to-all-done.1.states_ref = bf16[8,512,128]{2,1,0:T(8,128)(2,1)} async-done(((bf16[8,512,128]{2,1,0:T(8,128)(2,1)}), bf16[8,512,128]{2,1,0:T(8,128)(2,1)}, u32[]{:S(2)}, u32[]{:S(2)}) %all-to-all-start.1) | async-done | bytes 1048608 | tf_op jit(solution)/shard_map/all_to_all | solution.py:399
  22.3 0.0 copy-done.9
  22.3 7.2 %all-to-all-start = ((bf16[8,544,128]{2,1,0:T(8,128)(2,1)}), bf16[8,544,128]{2,1,0:T(8,128)(2,1)}, u32[]{:S(2)}, u32[]{:S(2)}) async-start(bf16[8,544,128]{2,1,0:T(8,128)(2,1)} %pad_maximum_fusion), calls=%async_computation | async-start | bytes 2228224 | tf_op jit(solution)/shard_map/all_to_all | solution.py:408
  29.5 0.0 copy-start.3
  29.5 0.0 copy-start.11
  29.5 11.8 %teacher.1.q_hbm = bf16[2064,512]{1,0:T(8,128)(2,1)} custom-call(s32[16]{0:T(128)} %start_ref.3, bf16[8,512,128]{2,1,0:T(8,128)(2,1)} %all-to-all-done.1.states_ref, f32[128,8,128]{2,1,0:T(8,128)} %copy-done.10, bf16[1024,1024]{1,0:T(8,128)(2,1)} %weight_ref.1, bf16[1024,512]{1,0:T(8,128)(2,1)} %copy-done.9), custom_call_target="tpu_custom_call" | custom-call | flops 42949672960 | bytes 8388608 | tf_op jit(solution)/shard_map/teacher/pallas_call | solution.py:186
  41.3 0.0 collective-permute-done.before_ref
  41.3 4.5 %all-to-all-done.arrived_ref = bf16[8,544,128]{2,1,0:T(8,128)(2,1)} async-done(((bf16[8,544,128]{2,1,0:T(8,128)(2,1)}), bf16[8,544,128]{2,1,0:T(8,128)(2,1)}, u32[]{:S(2)}, u32[]{:S(2)}) %all-to-all-start) | async-done | bytes 1114144 | tf_op jit(solution)/shard_map/all_to_all | solution.py:408
  45.8 0.0 copy-done.3
  45.8 0.0 copy-done.11
  45.8 6.8 %student.1 = f32[16,8,128]{2,1,0:T(8,128)S(1)} custom-call(s32[16]{0:T(128)S(1)} %copy-done.11, s32[1]{0:T(128)} %bitcast.core_ref, s32[128]{0:T(128)S(1)} %copy-done.7, s32[128]{0:T(128)S(1)} %copy-done.8, s32[2,2]{1,0:T(2,128)S(1)} %collective-permute-done.before_ref, bf16[8,544,128]{2,1,0:T(8,128)(2,1)} %all-to-all-done.arrived_ref, ...), custom_call_target="tpu_custom_call" | custom-call | flops 2147483648 | bytes 6291456 | tf_op jit(solution)/shard_map/student/pallas_call | solution.py:322
  52.6 12.6 %all_to_all.15.answers_ref = f32[16,8,128]{2,1,0:T(8,128)S(1)} all-to-all(f32[16,8,128]{2,1,0:T(8,128)S(1)} %student.1), channel_id=1, replica_groups=mesh['frames'=16,'mp'=8] {'frames'}, dimensions={0} | all-to-all | bytes 131072 | tf_op jit(solution)/shard_map/all_to_all | solution.py:419
  65.2 1.4 %pick.1 = f32[16,4,32]{2,1,0:T(4,128)} custom-call(s32[1,16]{1,0:T(1,128)S(1)} %copy-done.6, f32[16,8,128]{2,1,0:T(8,128)S(1)} %all_to_all.15.answers_ref), custom_call_target="tpu_custom_call" | custom-call | tf_op jit(solution)/shard_map/pick/pallas_call | solution.py:369
  (1 shorter events, 0.0 us)
Async XLA Ops:
  0.0 6.4 %copy-start.7 = (s32[128]{0:T(128)S(1)}, s32[128]{0:T(128)}, u32[]{:S(2)}) copy-start(s32[128]{0:T(128)} %labels_ref.1) | copy-start | bytes 1540
  0.0 6.4 %copy-start.8 = (s32[128]{0:T(128)S(1)}, s32[128]{0:T(128)}, u32[]{:S(2)}) copy-start(s32[128]{0:T(128)} %utt_ref.1) | copy-start | bytes 1540
  0.0 6.4 %copy-start = (bf16[1024,512]{1,0:T(8,128)(2,1)S(1)}, bf16[1024,512]{1,0:T(8,128)(2,1)}, u32[]{:S(2)}) copy-start(bf16[1024,512]{1,0:T(8,128)(2,1)} %last_hbm.1) | copy-start | bytes 3145732
  0.0 6.4 %copy-start.1 = (bf16[1024,512]{1,0:T(8,128)(2,1)S(1)}, bf16[1024,512]{1,0:T(8,128)(2,1)}, u32[]{:S(2)}) copy-start(bf16[1024,512]{1,0:T(8,128)(2,1)} %second_hbm.1) | copy-start | bytes 3145732
  0.0 6.4 %copy-start.6 = (s32[1,16]{1,0:T(1,128)S(1)}, s32[1,16]{1,0:T(1,128)}, u32[]{:S(2)}) copy-start(s32[1,16]{1,0:T(1,128)} %list_ref.3) | copy-start | bytes 196
  0.0 22.3 %all-to-all-start.1 = ((bf16[8,512,128]{2,1,0:T(8,128)(2,1)}), bf16[8,512,128]{2,1,0:T(8,128)(2,1)}, u32[]{:S(2)}, u32[]{:S(2)}) async-start(bf16[8,512,128]{2,1,0:T(8,128)(2,1)} %bitcast.10), calls=%async_computation.1 | async-start | bytes 2097152 | tf_op jit(solution)/shard_map/all_to_all | solution.py:399
  6.4 1.2 %copy-start.2 = (bf16[512,1024]{1,0:T(8,128)(2,1)S(1)}, bf16[512,1024]{1,0:T(8,128)(2,1)}, u32[]{:S(2)}) copy-start(bf16[512,1024]{1,0:T(8,128)(2,1)} %weight_hbm.1) | copy-start | bytes 3145732
  7.7 1.0 %copy-start.4 = (bf16[512,512]{1,0:T(8,128)(2,1)S(1)}, bf16[512,512]{1,0:T(8,128)(2,1)}, u32[]{:S(2)}) copy-start(bf16[512,512]{1,0:T(8,128)(2,1)} %states_ref.1) | copy-start | bytes 1572868
  8.7 0.9 %copy-start.5 = (bf16[128,1024]{1,0:T(8,128)(2,1)S(1)}, bf16[128,1024]{1,0:T(8,128)(2,1)}, u32[]{:S(2)}) copy-start(bf16[128,1024]{1,0:T(8,128)(2,1)} %teacher_pred_ref.1) | copy-start | bytes 786436
  11.9 0.8 %copy-start.10 = (f32[128,8,128]{2,1,0:T(8,128)}, f32[128,8,128]{2,1,0:T(8,128)S(1)}, u32[]{:S(2)}) copy-start(f32[128,8,128]{2,1,0:T(8,128)S(1)} %get-tuple-element.13.pred_ref) | copy-start | bytes 1572868
  12.8 9.5 %copy-start.9 = (bf16[1024,512]{1,0:T(8,128)(2,1)}, bf16[1024,512]{1,0:T(8,128)(2,1)S(1)}, u32[]{:S(2)}) copy-start(bf16[1024,512]{1,0:T(8,128)(2,1)S(1)} %get-tuple-element.14.student_ref) | copy-start | bytes 3145732
  12.8 4.7 %collective-permute-start.1 = (bf16[8,272,128]{2,1,0:T(8,128)(2,1)S(1)}, bf16[8,272,128]{2,1,0:T(8,128)(2,1)S(1)}, u32[]{:S(2)}, u32[]{:S(2)}) collective-permute-start(bf16[8,272,128]{2,1,0:T(8,128)(2,1)S(1)} %get-tuple-element.11), channel_id=1, source_target_pairs={{0,8},{8,0},{16,24},{24,16},{32,40},{40,32},{48,56},{56,48},{64,72... | collective-permute-start | bytes 1671176 | tf_op jit(solution)/shard_map/ppermute | solution.py:407
  13.8 27.5 %collective-permute-start = (s32[2,2]{1,0:T(2,128)S(1)}, s32[2,2]{1,0:T(2,128)S(1)}, u32[]{:S(2)}, u32[]{:S(2)}) collective-permute-start(s32[2,2]{1,0:T(2,128)S(1)} %pad_add_fusion), channel_id=1, source_target_pairs={{0,1},{1,2},{2,3},{3,4},{4,5},{5,6},{6,7},{7,8},{8,9},{9,10},{10,1... | collective-permute-start | bytes 56 | tf_op jit(solution)/shard_map/ppermute | solution.py:22
  22.3 23.5 %all-to-all-start = ((bf16[8,544,128]{2,1,0:T(8,128)(2,1)}), bf16[8,544,128]{2,1,0:T(8,128)(2,1)}, u32[]{:S(2)}, u32[]{:S(2)}) async-start(bf16[8,544,128]{2,1,0:T(8,128)(2,1)} %pad_maximum_fusion), calls=%async_computation | async-start | bytes 2228224 | tf_op jit(solution)/shard_map/all_to_all | solution.py:408
  29.5 16.3 %copy-start.3 = (bf16[512,1024]{1,0:T(8,128)(2,1)S(1)}, bf16[512,1024]{1,0:T(8,128)(2,1)}, u32[]{:S(2)}) copy-start(bf16[512,1024]{1,0:T(8,128)(2,1)} %weight_hbm.1) | copy-start | bytes 3145732
  29.5 16.3 %copy-start.11 = (s32[16]{0:T(128)S(1)}, s32[16]{0:T(128)}, u32[]{:S(2)}) copy-start(s32[16]{0:T(128)} %start_ref.3) | copy-start | bytes 196

commit v4 on v3

--- a/solution.py
+++ b/solution.py
@@ -116,7 +116,7 @@
         in_specs=[smem(), smem()] + [vmem()] * 7,
         out_specs=(vmem(),) * 5,
         scratch_shapes=[pltpu.SMEM((frame_peers,), jnp.int32), pltpu.VMEM((label_count, words), BF16)],
-        compiler_params=pltpu.CompilerParams(vmem_limit_bytes=16 << 20),
+        compiler_params=pltpu.CompilerParams(vmem_limit_bytes=56 << 20),
         cost_estimate=pl.CostEstimate(flops=0, bytes_accessed=3 << 20, transcendentals=0),
         name="pack",
     )(block_list, core, student_states, labels, label_utt, embed_last, embed_second, teacher_pred, student_out)
@@ -242,14 +242,14 @@
                 words.append(word - around)
                 copies.insert(n, pltpu.make_async_copy(table.at[pl.ds(around, TAG_ROWS), :], entries.at[n], sems.at[4 + n]))
         *first_copies, weight_copy, q_copy = copies
-        for each in copies:
-            each.start()
         for peer in range(peers):
             at = peer % CORES * message + CAP * slot_rows
             tile = arrived_ref[peer // CORES, at : at + TAG_ROWS, :].astype(F32)
             tags[peer : peer + 1, :] = tile[:1, :].astype(jnp.int32)
         copy = pltpu.make_async_copy(tags, tag_smem, sems.at[0])
         copy.start()
+        for each in copies:
+            each.start()
         copy.wait()
         for peer in range(peers):
             for slot in range(CAP):

time: 67 us -> 66.7 us (level)
  local copies, waits for them, and re-layouts: 4.13 us -> 0.12 us
  Pallas kernels: 22.2 us -> 25.4 us
  other arithmetic: 1.08 us -> 2.14 us
    unnamed x24 -> x18, local copies, waits for them, and re-layouts: 4.05 us -> 0.05 us
    pallas_call x1, Pallas kernels: 2.28 us -> 5.53 us  [pack(): pl.pallas_call(body, out_shape=(jax.ShapeDtypeStruct((chips, message, LAN...]
    concatenate x1, other arithmetic: 1.06 us -> 2.12 us  [shards(): jnp.concatenate([own, other], axis=1)]
  transfers between devices with their start and end apart: 4 -> 4, of which waited for: 2 -> 2; matrix products, arithmetic and copies ran while one was open for 2% -> 3% of each run, Pallas kernels for 21% -> 26%
where the time goes in v4:
time: 66.7 us; the launch traced here: 66.3 us
  Pallas kernels  25.4 us (38%)
  starting transfers between devices  18 us (27%)
  blocking collectives  12.6 us (19%)
  waiting for transfers between devices  7.85 us (12%)
  other arithmetic  2.14 us (3%)
    all_to_all x1, blocking collectives, shards(): returned = lax.all_to_all(answers, 'frames', split_axis=0, concat_axis=0)  12.6 us
    pallas_call x1, Pallas kernels, teacher(): pl.pallas_call(body, out_shape=jax.ShapeDtypeStruct((total_rows + count,...  11.8 us
    all_to_all x1, starting transfers between devices, shards(): lax.all_to_all(jnp.concatenate([own, other], axis=1), 'frames', split_axi...  7.21 us
    pallas_call x1, Pallas kernels, student(): pl.pallas_call(body, out_shape=jax.ShapeDtypeStruct((peers, 8, LANES), F3...  6.72 us
    all_to_all x1, starting transfers between devices, shards(): lax.all_to_all(teacher_states.reshape(mp_peers, -1, teacher_states.shape[...  6.2 us
    pallas_call x1, Pallas kernels, pack(): pl.pallas_call(body, out_shape=(jax.ShapeDtypeStruct((chips, message, LAN...  5.53 us
    all_to_all x1, waiting for transfers between devices, shards(): lax.all_to_all(jnp.concatenate([own, other], axis=1), 'frames', split_axi...  4.42 us
    ppermute x1, starting transfers between devices, shifted_2(): return lax.ppermute(block, axis, route)  3.64 us
  transfers between devices with their start and end apart: 4, of which 2 were waited for; matrix products, arithmetic and copies ran while one was open for 3% of the time, Pallas kernels for 26%

profile of v4, /device:TPU:1, one launch (start us, length us, event | category | flops | bytes accessed | tf_op | source)
XLA Modules:
  0.0 66.3 jit_solution(8945811725219773913)
XLA Ops:
  0.0 6.2 %all-to-all-start.1 = ((bf16[8,512,128]{2,1,0:T(8,128)(2,1)}), bf16[8,512,128]{2,1,0:T(8,128)(2,1)S(1)}, u32[]{:S(2)}, u32[]{:S(2)}) async-start(bf16[8,512,128]{2,1,0:T(8,128)(2,1)} %bitcast.10), calls=%async_computation.1 | async-start | bytes 2097152 | tf_op jit(solution)/shard_map/all_to_all | solution.py:399
  6.2 0.0 copy-start.4
  6.2 0.0 copy-start.5
  6.2 5.5 %pack.1 = (bf16[8,272,128]{2,1,0:T(8,128)(2,1)}, bf16[8,272,128]{2,1,0:T(8,128)(2,1)}, f32[128,4,128]{2,1,0:T(4,128)}, f32[128,8,128]{2,1,0:T(8,128)}, bf16[1024,512]{1,0:T(8,128)(2,1)}) custom-call(s32[1,16]{1,0:T(1,128)} %list_ref.3, s32[1]{0:T(128)} %bitcast.core_ref, bf16[512,512]{1,0:T(8,128)(2,1)} %states_ref.1, s32[1,128]{1,0:T(1,128)} %bitcast.8, ...), custom_call_target="tpu_custom_call" | custom-call | bytes 3145728 | tf_op jit(solution)/shard_map/pack/pallas_call | solution.py:108
  11.8 1.0 %collective-permute-start.1 = (bf16[8,272,128]{2,1,0:T(8,128)(2,1)}, bf16[8,272,128]{2,1,0:T(8,128)(2,1)S(1)}, u32[]{:S(2)}, u32[]{:S(2)}) collective-permute-start(bf16[8,272,128]{2,1,0:T(8,128)(2,1)} %get-tuple-element.11), channel_id=1, source_target_pairs={{0,8},{8,0},{16,24},{24,16},{32,40},{40,32},{48,56},{56,48},{64,72... | collective-permute-start | bytes 1671176 | tf_op jit(solution)/shard_map/ppermute | solution.py:407
  12.7 0.0 copy-done.4
  12.7 0.0 copy-done.5
  12.7 0.1 slice_bitcast_fusion
  12.8 3.6 %collective-permute-start = (s32[2,2]{1,0:T(2,128)S(1)}, s32[2,2]{1,0:T(2,128)S(1)}, u32[]{:S(2)}, u32[]{:S(2)}) collective-permute-start(s32[2,2]{1,0:T(2,128)S(1)} %pad_add_fusion), channel_id=1, source_target_pairs={{0,1},{1,2},{2,3},{3,4},{4,5},{5,6},{6,7},{7,8},{8,9},{9,10},{10,1... | collective-permute-start | bytes 56 | tf_op jit(solution)/shard_map/ppermute | solution.py:22
  16.5 0.0 collective-permute-done.1
  16.5 2.1 %pad_maximum_fusion = bf16[8,544,128]{2,1,0:T(8,128)(2,1)} fusion(bf16[8,272,128]{2,1,0:T(8,128)(2,1)S(1)} %collective-permute-done.1, bf16[8,272,128]{2,1,0:T(8,128)(2,1)} %get-tuple-element.10), kind=kLoop, calls=%fused_computation | loop fusion | flops 2228224 | bytes 2228224 | tf_op jit(solution)/shard_map/concatenate | solution.py:409
  18.6 3.4 %all-to-all-done.1.states_ref = bf16[8,512,128]{2,1,0:T(8,128)(2,1)S(1)} async-done(((bf16[8,512,128]{2,1,0:T(8,128)(2,1)}), bf16[8,512,128]{2,1,0:T(8,128)(2,1)S(1)}, u32[]{:S(2)}, u32[]{:S(2)}) %all-to-all-start.1) | async-done | bytes 1048608 | tf_op jit(solution)/shard_map/all_to_all | solution.py:399
  22.0 0.0 copy-start.8
  22.0 7.2 %all-to-all-start = ((bf16[8,544,128]{2,1,0:T(8,128)(2,1)}), bf16[8,544,128]{2,1,0:T(8,128)(2,1)}, u32[]{:S(2)}, u32[]{:S(2)}) async-start(bf16[8,544,128]{2,1,0:T(8,128)(2,1)} %pad_maximum_fusion), calls=%async_computation | async-start | bytes 2228224 | tf_op jit(solution)/shard_map/all_to_all | solution.py:408
  29.2 0.0 copy-done.8
  29.2 0.0 copy-start
  29.2 0.0 copy-start.1
  29.3 0.0 copy-start.2
  29.3 0.0 copy-start.6
  29.3 0.0 copy-start.7
  29.3 11.8 %teacher.1.q_hbm = bf16[2064,512]{1,0:T(8,128)(2,1)} custom-call(s32[16]{0:T(128)} %start_ref.3, bf16[8,512,128]{2,1,0:T(8,128)(2,1)} %copy-done.8, f32[128,8,128]{2,1,0:T(8,128)} %get-tuple-element.13.pred_ref, bf16[1024,1024]{1,0:T(8,128)(2,1)} %weight_ref.1, bf16[1024,512]{1,0:T(8,128)(2,1)} %get-tuple-element.14.student_ref), custom_call_target="tpu_custom_call" | custom-call | flops 42949672960 | bytes 8388608 | tf_op jit(solution)/shard_map/teacher/pallas_call | solution.py:186
  41.1 0.0 collective-permute-done.before_ref
  41.1 4.4 %all-to-all-done.arrived_ref = bf16[8,544,128]{2,1,0:T(8,128)(2,1)} async-done(((bf16[8,544,128]{2,1,0:T(8,128)(2,1)}), bf16[8,544,128]{2,1,0:T(8,128)(2,1)}, u32[]{:S(2)}, u32[]{:S(2)}) %all-to-all-start) | async-done | bytes 1114144 | tf_op jit(solution)/shard_map/all_to_all | solution.py:408
  45.5 0.0 copy-done
  45.6 0.0 copy-done.1
  45.6 0.0 copy-done.2
  45.6 0.0 copy-done.6
  45.6 0.0 copy-done.7
  45.6 0.0 copy-start.3
  45.6 6.7 %student.1 = f32[16,8,128]{2,1,0:T(8,128)S(1)} custom-call(s32[16]{0:T(128)S(1)} %copy-done.7, s32[1]{0:T(128)} %bitcast.core_ref, s32[128]{0:T(128)S(1)} %copy-done.4, s32[128]{0:T(128)S(1)} %copy-done.5, s32[2,2]{1,0:T(2,128)S(1)} %collective-permute-done.before_ref, bf16[8,544,128]{2,1,0:T(8,128)(2,1)} %all-to-all-done.arrived_ref, ...), custom_call_target="tpu_custom_call" | custom-call | flops 2147483648 | bytes 6291456 | tf_op jit(solution)/shard_map/student/pallas_call | solution.py:322
  52.3 12.6 %all_to_all.15.answers_ref = f32[16,8,128]{2,1,0:T(8,128)S(1)} all-to-all(f32[16,8,128]{2,1,0:T(8,128)S(1)} %student.1), channel_id=1, replica_groups=mesh['frames'=16,'mp'=8] {'frames'}, dimensions={0} | all-to-all | bytes 131072 | tf_op jit(solution)/shard_map/all_to_all | solution.py:419
  64.9 0.0 copy-done.3
  64.9 1.4 %pick.1 = f32[16,4,32]{2,1,0:T(4,128)} custom-call(s32[1,16]{1,0:T(1,128)S(1)} %copy-done.3, f32[16,8,128]{2,1,0:T(8,128)S(1)} %all_to_all.15.answers_ref), custom_call_target="tpu_custom_call" | custom-call | tf_op jit(solution)/shard_map/pick/pallas_call | solution.py:369
  (1 shorter events, 0.0 us)
Async XLA Ops:
  0.0 22.0 %all-to-all-start.1 = ((bf16[8,512,128]{2,1,0:T(8,128)(2,1)}), bf16[8,512,128]{2,1,0:T(8,128)(2,1)S(1)}, u32[]{:S(2)}, u32[]{:S(2)}) async-start(bf16[8,512,128]{2,1,0:T(8,128)(2,1)} %bitcast.10), calls=%async_computation.1 | async-start | bytes 2097152 | tf_op jit(solution)/shard_map/all_to_all | solution.py:399
  6.2 6.5 %copy-start.4 = (s32[128]{0:T(128)S(1)}, s32[128]{0:T(128)}, u32[]{:S(2)}) copy-start(s32[128]{0:T(128)} %labels_ref.1) | copy-start | bytes 1540
  6.2 6.5 %copy-start.5 = (s32[128]{0:T(128)S(1)}, s32[128]{0:T(128)}, u32[]{:S(2)}) copy-start(s32[128]{0:T(128)} %utt_ref.1) | copy-start | bytes 1540
  11.8 4.7 %collective-permute-start.1 = (bf16[8,272,128]{2,1,0:T(8,128)(2,1)}, bf16[8,272,128]{2,1,0:T(8,128)(2,1)S(1)}, u32[]{:S(2)}, u32[]{:S(2)}) collective-permute-start(bf16[8,272,128]{2,1,0:T(8,128)(2,1)} %get-tuple-element.11), channel_id=1, source_target_pairs={{0,8},{8,0},{16,24},{24,16},{32,40},{40,32},{48,56},{56,48},{64,72... | collective-permute-start | bytes 1671176 | tf_op jit(solution)/shard_map/ppermute | solution.py:407
  12.8 28.3 %collective-permute-start = (s32[2,2]{1,0:T(2,128)S(1)}, s32[2,2]{1,0:T(2,128)S(1)}, u32[]{:S(2)}, u32[]{:S(2)}) collective-permute-start(s32[2,2]{1,0:T(2,128)S(1)} %pad_add_fusion), channel_id=1, source_target_pairs={{0,1},{1,2},{2,3},{3,4},{4,5},{5,6},{6,7},{7,8},{8,9},{9,10},{10,1... | collective-permute-start | bytes 56 | tf_op jit(solution)/shard_map/ppermute | solution.py:22
  22.0 7.2 %copy-start.8 = (bf16[8,512,128]{2,1,0:T(8,128)(2,1)}, bf16[8,512,128]{2,1,0:T(8,128)(2,1)S(1)}, u32[]{:S(2)}) copy-start(bf16[8,512,128]{2,1,0:T(8,128)(2,1)S(1)} %all-to-all-done.1.states_ref) | copy-start | bytes 3145732
  22.0 23.5 %all-to-all-start = ((bf16[8,544,128]{2,1,0:T(8,128)(2,1)}), bf16[8,544,128]{2,1,0:T(8,128)(2,1)}, u32[]{:S(2)}, u32[]{:S(2)}) async-start(bf16[8,544,128]{2,1,0:T(8,128)(2,1)} %pad_maximum_fusion), calls=%async_computation | async-start | bytes 2228224 | tf_op jit(solution)/shard_map/all_to_all | solution.py:408
  29.2 16.3 %copy-start = (bf16[1024,512]{1,0:T(8,128)(2,1)S(1)}, bf16[1024,512]{1,0:T(8,128)(2,1)}, u32[]{:S(2)}) copy-start(bf16[1024,512]{1,0:T(8,128)(2,1)} %last_hbm.1) | copy-start | bytes 3145732
  29.2 16.3 %copy-start.1 = (bf16[1024,512]{1,0:T(8,128)(2,1)S(1)}, bf16[1024,512]{1,0:T(8,128)(2,1)}, u32[]{:S(2)}) copy-start(bf16[1024,512]{1,0:T(8,128)(2,1)} %second_hbm.1) | copy-start | bytes 3145732
  29.3 16.3 %copy-start.2 = (bf16[512,1024]{1,0:T(8,128)(2,1)S(1)}, bf16[512,1024]{1,0:T(8,128)(2,1)}, u32[]{:S(2)}) copy-start(bf16[512,1024]{1,0:T(8,128)(2,1)} %weight_hbm.1) | copy-start | bytes 3145732
  29.3 16.3 %copy-start.6 = (f32[128,4,128]{2,1,0:T(4,128)S(1)}, f32[128,4,128]{2,1,0:T(4,128)}, u32[]{:S(2)}) copy-start(f32[128,4,128]{2,1,0:T(4,128)} %get-tuple-element.12.pred_hbm) | copy-start | bytes 786436
  29.3 16.3 %copy-start.7 = (s32[16]{0:T(128)S(1)}, s32[16]{0:T(128)}, u32[]{:S(2)}) copy-start(s32[16]{0:T(128)} %start_ref.3) | copy-start | bytes 196
  45.6 19.4 %copy-start.3 = (s32[1,16]{1,0:T(1,128)S(1)}, s32[1,16]{1,0:T(1,128)}, u32[]{:S(2)}) copy-start(s32[1,16]{1,0:T(1,128)} %list_ref.3) | copy-start | bytes 196

commit v5 on v4

--- a/solution.py
+++ b/solution.py
@@ -12,6 +12,7 @@
 CORES = 2
 PARTS = 3
 GROUP = 2
+STUDENT_GROUP = 4
 BF16 = jnp.bfloat16
 F32 = jnp.float32
 
@@ -214,8 +215,8 @@
     slot_rows = (message - TAG_ROWS) // CAP
     block_rows = slot_rows // pieces
     out_block = S * block_rows
-    step_rows = GROUP * out_block
-    steps = count // GROUP
+    step_rows = STUDENT_GROUP * out_block
+    steps = count // STUDENT_GROUP
     total_rows = count * out_block
     assert out_block == LANES
 
@@ -269,7 +270,7 @@
                 pred_ref[at, piece : piece + 1, :] = first_rows[:, piece * LANES : (piece + 1) * LANES]
 
         def activate(step):
-            for block in range(step * GROUP, (step + 1) * GROUP):
+            for block in range(step * STUDENT_GROUP, (step + 1) * STUDENT_GROUP):
                 first = start_ref[block]
                 place = where[block]
                 chip = place // (CORES * CAP)
@@ -292,7 +293,7 @@
         def normalise(step):
             if step == 0:
                 q_copy.wait()
-            for block in range(step * GROUP, (step + 1) * GROUP):
+            for block in range(step * STUDENT_GROUP, (step + 1) * STUDENT_GROUP):
                 at = slice(block * out_block, (block + 1) * out_block)
                 values = logits[at, :]
                 largest = jnp.max(values, axis=-1, keepdims=True)

time: 66.7 us -> 66.6 us (level)
  no operation moved by 1% of the time
where the time goes in v5:
time: 66.6 us; the launch traced here: 66.2 us
  Pallas kernels  25.4 us (38%)
  starting transfers between devices  18 us (27%)
  blocking collectives  12.6 us (19%)
  waiting for transfers between devices  7.85 us (12%)
  other arithmetic  2.14 us (3%)
    all_to_all x1, blocking collectives, shards(): returned = lax.all_to_all(answers, 'frames', split_axis=0, concat_axis=0)  12.6 us
    pallas_call x1, Pallas kernels, teacher(): pl.pallas_call(body, out_shape=jax.ShapeDtypeStruct((total_rows + count,...  11.8 us
    all_to_all x1, starting transfers between devices, shards(): lax.all_to_all(jnp.concatenate([own, other], axis=1), 'frames', split_axi...  7.21 us
    pallas_call x1, Pallas kernels, student(): pl.pallas_call(body, out_shape=jax.ShapeDtypeStruct((peers, 8, LANES), F3...  6.63 us
    all_to_all x1, starting transfers between devices, shards(): lax.all_to_all(teacher_states.reshape(mp_peers, -1, teacher_states.shape[...  6.2 us
    pallas_call x1, Pallas kernels, pack(): pl.pallas_call(body, out_shape=(jax.ShapeDtypeStruct((chips, message, LAN...  5.53 us
    all_to_all x1, waiting for transfers between devices, shards(): lax.all_to_all(jnp.concatenate([own, other], axis=1), 'frames', split_axi...  4.41 us
    ppermute x1, starting transfers between devices, shifted_2(): return lax.ppermute(block, axis, route)  3.64 us
  transfers between devices with their start and end apart: 4, of which 2 were waited for; matrix products, arithmetic and copies ran while one was open for 3% of the time, Pallas kernels for 26%

profile of v5, /device:TPU:1, one launch (start us, length us, event | category | flops | bytes accessed | tf_op | source)
XLA Modules:
  0.0 66.2 jit_solution(10308889907922655110)
XLA Ops:
  0.0 6.2 %all-to-all-start.1 = ((bf16[8,512,128]{2,1,0:T(8,128)(2,1)}), bf16[8,512,128]{2,1,0:T(8,128)(2,1)S(1)}, u32[]{:S(2)}, u32[]{:S(2)}) async-start(bf16[8,512,128]{2,1,0:T(8,128)(2,1)} %bitcast.10), calls=%async_computation.1 | async-start | bytes 2097152 | tf_op jit(solution)/shard_map/all_to_all | solution.py:400
  6.2 0.0 copy-start.4
  6.2 0.0 copy-start.5
  6.2 5.5 %pack.1 = (bf16[8,272,128]{2,1,0:T(8,128)(2,1)}, bf16[8,272,128]{2,1,0:T(8,128)(2,1)}, f32[128,4,128]{2,1,0:T(4,128)}, f32[128,8,128]{2,1,0:T(8,128)}, bf16[1024,512]{1,0:T(8,128)(2,1)}) custom-call(s32[1,16]{1,0:T(1,128)} %list_ref.3, s32[1]{0:T(128)} %bitcast.core_ref, bf16[512,512]{1,0:T(8,128)(2,1)} %states_ref.1, s32[1,128]{1,0:T(1,128)} %bitcast.8, ...), custom_call_target="tpu_custom_call" | custom-call | bytes 3145728 | tf_op jit(solution)/shard_map/pack/pallas_call | solution.py:109
  11.8 1.0 %collective-permute-start.1 = (bf16[8,272,128]{2,1,0:T(8,128)(2,1)}, bf16[8,272,128]{2,1,0:T(8,128)(2,1)S(1)}, u32[]{:S(2)}, u32[]{:S(2)}) collective-permute-start(bf16[8,272,128]{2,1,0:T(8,128)(2,1)} %get-tuple-element.11), channel_id=1, source_target_pairs={{0,8},{8,0},{16,24},{24,16},{32,40},{40,32},{48,56},{56,48},{64,72... | collective-permute-start | bytes 1671176 | tf_op jit(solution)/shard_map/ppermute | solution.py:408
  12.7 0.0 copy-done.4
  12.7 0.0 copy-done.5
  12.7 0.1 slice_bitcast_fusion
  12.8 3.6 %collective-permute-start = (s32[2,2]{1,0:T(2,128)S(1)}, s32[2,2]{1,0:T(2,128)S(1)}, u32[]{:S(2)}, u32[]{:S(2)}) collective-permute-start(s32[2,2]{1,0:T(2,128)S(1)} %pad_add_fusion), channel_id=1, source_target_pairs={{0,1},{1,2},{2,3},{3,4},{4,5},{5,6},{6,7},{7,8},{8,9},{9,10},{10,1... | collective-permute-start | bytes 56 | tf_op jit(solution)/shard_map/ppermute | solution.py:23
  16.5 0.0 collective-permute-done.1
  16.5 2.1 %pad_maximum_fusion = bf16[8,544,128]{2,1,0:T(8,128)(2,1)} fusion(bf16[8,272,128]{2,1,0:T(8,128)(2,1)S(1)} %collective-permute-done.1, bf16[8,272,128]{2,1,0:T(8,128)(2,1)} %get-tuple-element.10), kind=kLoop, calls=%fused_computation | loop fusion | flops 2228224 | bytes 2228224 | tf_op jit(solution)/shard_map/concatenate | solution.py:410
  18.6 3.4 %all-to-all-done.1.states_ref = bf16[8,512,128]{2,1,0:T(8,128)(2,1)S(1)} async-done(((bf16[8,512,128]{2,1,0:T(8,128)(2,1)}), bf16[8,512,128]{2,1,0:T(8,128)(2,1)S(1)}, u32[]{:S(2)}, u32[]{:S(2)}) %all-to-all-start.1) | async-done | bytes 1048608 | tf_op jit(solution)/shard_map/all_to_all | solution.py:400
  22.0 0.0 copy-start.8
  22.0 7.2 %all-to-all-start = ((bf16[8,544,128]{2,1,0:T(8,128)(2,1)}), bf16[8,544,128]{2,1,0:T(8,128)(2,1)}, u32[]{:S(2)}, u32[]{:S(2)}) async-start(bf16[8,544,128]{2,1,0:T(8,128)(2,1)} %pad_maximum_fusion), calls=%async_computation | async-start | bytes 2228224 | tf_op jit(solution)/shard_map/all_to_all | solution.py:409
  29.2 0.0 copy-done.8
  29.2 0.0 copy-start
  29.2 0.0 copy-start.1
  29.3 0.0 copy-start.2
  29.3 0.0 copy-start.6
  29.3 0.0 copy-start.7
  29.3 11.8 %teacher.1.q_hbm = bf16[2064,512]{1,0:T(8,128)(2,1)} custom-call(s32[16]{0:T(128)} %start_ref.3, bf16[8,512,128]{2,1,0:T(8,128)(2,1)} %copy-done.8, f32[128,8,128]{2,1,0:T(8,128)} %get-tuple-element.13.pred_ref, bf16[1024,1024]{1,0:T(8,128)(2,1)} %weight_ref.1, bf16[1024,512]{1,0:T(8,128)(2,1)} %get-tuple-element.14.student_ref), custom_call_target="tpu_custom_call" | custom-call | flops 42949672960 | bytes 8388608 | tf_op jit(solution)/shard_map/teacher/pallas_call | solution.py:187
  41.1 0.0 collective-permute-done.before_ref
  41.1 4.4 %all-to-all-done.arrived_ref = bf16[8,544,128]{2,1,0:T(8,128)(2,1)} async-done(((bf16[8,544,128]{2,1,0:T(8,128)(2,1)}), bf16[8,544,128]{2,1,0:T(8,128)(2,1)}, u32[]{:S(2)}, u32[]{:S(2)}) %all-to-all-start) | async-done | bytes 1114144 | tf_op jit(solution)/shard_map/all_to_all | solution.py:409
  45.5 0.0 copy-done
  45.6 0.0 copy-done.1
  45.6 0.0 copy-done.2
  45.6 0.0 copy-done.6
  45.6 0.0 copy-done.7
  45.6 0.0 copy-start.3
  45.6 6.6 %student.1 = f32[16,8,128]{2,1,0:T(8,128)S(1)} custom-call(s32[16]{0:T(128)S(1)} %copy-done.7, s32[1]{0:T(128)} %bitcast.core_ref, s32[128]{0:T(128)S(1)} %copy-done.4, s32[128]{0:T(128)S(1)} %copy-done.5, s32[2,2]{1,0:T(2,128)S(1)} %collective-permute-done.before_ref, bf16[8,544,128]{2,1,0:T(8,128)(2,1)} %all-to-all-done.arrived_ref, ...), custom_call_target="tpu_custom_call" | custom-call | flops 2147483648 | bytes 6291456 | tf_op jit(solution)/shard_map/student/pallas_call | solution.py:323
  52.2 12.6 %all_to_all.15.answers_ref = f32[16,8,128]{2,1,0:T(8,128)S(1)} all-to-all(f32[16,8,128]{2,1,0:T(8,128)S(1)} %student.1), channel_id=1, replica_groups=mesh['frames'=16,'mp'=8] {'frames'}, dimensions={0} | all-to-all | bytes 131072 | tf_op jit(solution)/shard_map/all_to_all | solution.py:420
  64.8 0.0 copy-done.3
  64.8 1.4 %pick.1 = f32[16,4,32]{2,1,0:T(4,128)} custom-call(s32[1,16]{1,0:T(1,128)S(1)} %copy-done.3, f32[16,8,128]{2,1,0:T(8,128)S(1)} %all_to_all.15.answers_ref), custom_call_target="tpu_custom_call" | custom-call | tf_op jit(solution)/shard_map/pick/pallas_call | solution.py:370
  (1 shorter events, 0.0 us)
Async XLA Ops:
  0.0 22.0 %all-to-all-start.1 = ((bf16[8,512,128]{2,1,0:T(8,128)(2,1)}), bf16[8,512,128]{2,1,0:T(8,128)(2,1)S(1)}, u32[]{:S(2)}, u32[]{:S(2)}) async-start(bf16[8,512,128]{2,1,0:T(8,128)(2,1)} %bitcast.10), calls=%async_computation.1 | async-start | bytes 2097152 | tf_op jit(solution)/shard_map/all_to_all | solution.py:400
  6.2 6.5 %copy-start.4 = (s32[128]{0:T(128)S(1)}, s32[128]{0:T(128)}, u32[]{:S(2)}) copy-start(s32[128]{0:T(128)} %labels_ref.1) | copy-start | bytes 1540
  6.2 6.5 %copy-start.5 = (s32[128]{0:T(128)S(1)}, s32[128]{0:T(128)}, u32[]{:S(2)}) copy-start(s32[128]{0:T(128)} %utt_ref.1) | copy-start | bytes 1540
  11.8 4.7 %collective-permute-start.1 = (bf16[8,272,128]{2,1,0:T(8,128)(2,1)}, bf16[8,272,128]{2,1,0:T(8,128)(2,1)S(1)}, u32[]{:S(2)}, u32[]{:S(2)}) collective-permute-start(bf16[8,272,128]{2,1,0:T(8,128)(2,1)} %get-tuple-element.11), channel_id=1, source_target_pairs={{0,8},{8,0},{16,24},{24,16},{32,40},{40,32},{48,56},{56,48},{64,72... | collective-permute-start | bytes 1671176 | tf_op jit(solution)/shard_map/ppermute | solution.py:408
  12.8 28.3 %collective-permute-start = (s32[2,2]{1,0:T(2,128)S(1)}, s32[2,2]{1,0:T(2,128)S(1)}, u32[]{:S(2)}, u32[]{:S(2)}) collective-permute-start(s32[2,2]{1,0:T(2,128)S(1)} %pad_add_fusion), channel_id=1, source_target_pairs={{0,1},{1,2},{2,3},{3,4},{4,5},{5,6},{6,7},{7,8},{8,9},{9,10},{10,1... | collective-permute-start | bytes 56 | tf_op jit(solution)/shard_map/ppermute | solution.py:23
  22.0 7.2 %copy-start.8 = (bf16[8,512,128]{2,1,0:T(8,128)(2,1)}, bf16[8,512,128]{2,1,0:T(8,128)(2,1)S(1)}, u32[]{:S(2)}) copy-start(bf16[8,512,128]{2,1,0:T(8,128)(2,1)S(1)} %all-to-all-done.1.states_ref) | copy-start | bytes 3145732
  22.0 23.5 %all-to-all-start = ((bf16[8,544,128]{2,1,0:T(8,128)(2,1)}), bf16[8,544,128]{2,1,0:T(8,128)(2,1)}, u32[]{:S(2)}, u32[]{:S(2)}) async-start(bf16[8,544,128]{2,1,0:T(8,128)(2,1)} %pad_maximum_fusion), calls=%async_computation | async-start | bytes 2228224 | tf_op jit(solution)/shard_map/all_to_all | solution.py:409
  29.2 16.3 %copy-start = (bf16[1024,512]{1,0:T(8,128)(2,1)S(1)}, bf16[1024,512]{1,0:T(8,128)(2,1)}, u32[]{:S(2)}) copy-start(bf16[1024,512]{1,0:T(8,128)(2,1)} %last_hbm.1) | copy-start | bytes 3145732
  29.2 16.3 %copy-start.1 = (bf16[1024,512]{1,0:T(8,128)(2,1)S(1)}, bf16[1024,512]{1,0:T(8,128)(2,1)}, u32[]{:S(2)}) copy-start(bf16[1024,512]{1,0:T(8,128)(2,1)} %second_hbm.1) | copy-start | bytes 3145732
  29.3 16.3 %copy-start.2 = (bf16[512,1024]{1,0:T(8,128)(2,1)S(1)}, bf16[512,1024]{1,0:T(8,128)(2,1)}, u32[]{:S(2)}) copy-start(bf16[512,1024]{1,0:T(8,128)(2,1)} %weight_hbm.1) | copy-start | bytes 3145732
  29.3 16.3 %copy-start.6 = (f32[128,4,128]{2,1,0:T(4,128)S(1)}, f32[128,4,128]{2,1,0:T(4,128)}, u32[]{:S(2)}) copy-start(f32[128,4,128]{2,1,0:T(4,128)} %get-tuple-element.12.pred_hbm) | copy-start | bytes 786436
  29.3 16.3 %copy-start.7 = (s32[16]{0:T(128)S(1)}, s32[16]{0:T(128)}, u32[]{:S(2)}) copy-start(s32[16]{0:T(128)} %start_ref.3) | copy-start | bytes 196
  45.6 19.2 %copy-start.3 = (s32[1,16]{1,0:T(1,128)S(1)}, s32[1,16]{1,0:T(1,128)}, u32[]{:S(2)}) copy-start(s32[1,16]{1,0:T(1,128)} %list_ref.3) | copy-start | bytes 196
